TPU v7x, 32 devices: a whole 2x2x4 slice. The times are simulated.
32 devices in a mesh: layer: 2 (over x), latent: 8 (over z, y), tok: 2 (over core).
Axes of the slice: x: 2, y: 2, z: 4, core: 2. Of those that a mesh axis runs over, the one named last changes fastest.
Arguments:
- activations: bfloat16 [2, 1280, 3584], P('layer', 'tok'), may hold values from -6 to 6
- enc_weight: bfloat16 [2, 3584, 8192], P('layer', 'tok', 'latent'), may hold values from -0.0625 to 0.0625
- enc_bias: float32 [8192], P('latent'), may hold values from -3 to 3
- dec_weight: bfloat16 [8192, 2, 3584], P('latent', 'layer', 'tok'), may hold values from -0.110485435 to 0.110485435
- dec_bias: float32 [2, 3584], P('layer'), may hold values from -3 to 3
Outputs:
- grad_enc: bfloat16 [2, 3584, 8192], P('layer', 'tok', 'latent')
- grad_dec: bfloat16 [8192, 2, 3584], P('latent', 'layer', 'tok')
All inputs are finite; a program needn't handle non-finite values.
Results may differ from a plain program's by a relative error of at most 0.023.
Values may be sent and summed in bfloat16 or wider, within the bound.
A program may use at most 128 MiB of HBM per device.

v0:
```python
import math

import jax
import jax.numpy as jnp
from jax import lax
from jax.sharding import PartitionSpec as P

LAMBDA = 1.0
EPSILON = 1e-06


def on_device(activations, enc_weight, enc_bias, dec_weight, dec_bias):
    tok_rows = activations[0]
    row_count = tok_rows.shape[0]
    loss_scale = 1.0 / math.sqrt(row_count * lax.axis_size("tok"))
    columns = tok_rows
    encoded = jnp.dot(
        columns,
        lax.all_gather(enc_weight, "tok", axis=1, tiled=True)[0],
        preferred_element_type=jnp.float32,
    )
    decoder = lax.all_gather(dec_weight, "tok", axis=2, tiled=True)
    dec_matrix = decoder[:, 0, :]
    half_sq = jnp.sum(jnp.square(dec_weight.astype(jnp.float32)), axis=(1, 2))
    norm_sq = lax.psum(half_sq, ("layer", "tok"))
    preact = lax.psum(encoded.astype(jnp.bfloat16), "layer").astype(jnp.float32)
    preact = preact + enc_bias
    positive = jnp.maximum(preact, 0.0)
    latents = (positive * positive).astype(jnp.bfloat16)
    partial_value = jnp.dot(latents, dec_matrix, preferred_element_type=jnp.float32)
    rebuilt = lax.psum(partial_value.astype(jnp.bfloat16), "latent").astype(jnp.float32)
    recon_error = (rebuilt + dec_bias[0] - tok_rows.astype(jnp.float32)).astype(jnp.bfloat16)
    back_part = lax.dot_general(
        recon_error, dec_matrix, (((1,), (1,)), ((), ())), preferred_element_type=jnp.float32
    )
    back_proj = lax.psum(back_part.astype(jnp.bfloat16), "layer").astype(jnp.float32)
    dec_norms = jnp.sqrt(norm_sq + EPSILON)
    pre_grad = (loss_scale * (back_proj + LAMBDA * dec_norms) * 2.0 * positive).astype(jnp.bfloat16)
    columns = tok_rows
    enc_summed = lax.psum_scatter(
        lax.dot_general(
            columns, pre_grad, (((0,), (0,)), ((), ())), preferred_element_type=jnp.float32
        ).astype(jnp.bfloat16),
        "tok",
        scatter_dimension=0,
        tiled=True,
    )
    grad_enc = enc_summed[None]
    col_totals = jnp.sum(latents.astype(jnp.float32), axis=0)
    dec_part = loss_scale * (
        lax.dot_general(
            latents, recon_error, (((0,), (0,)), ((), ())), preferred_element_type=jnp.float32
        )
        + LAMBDA * col_totals[:, None] * dec_matrix.astype(jnp.float32) / dec_norms[:, None]
    )
    dec_summed = lax.psum_scatter(
        dec_part[:, None, :].astype(jnp.bfloat16), "tok", scatter_dimension=2, tiled=True
    )
    return (grad_enc, dec_summed)


def solution(mesh):
    placed = (
        P("layer", "tok", None),
        P("layer", "tok", "latent"),
        P("latent"),
        P("latent", "layer", "tok"),
        P("layer", None),
    )
    return jax.shard_map(
        on_device,
        mesh=mesh,
        in_specs=placed,
        out_specs=(P("layer", "tok", "latent"), P("latent", "layer", "tok")),
        check_vma=False,
    )
```

profile of v0, /device:TPU:0, one launch (start us, length us, event | category | flops | bytes accessed | tf_op | source)
XLA Modules:
  0.0 389.3 jit_solution(10474185760495963353)
XLA Ops:
  7.2 0.7 all-gather.3.cloned.1.call-update
  7.9 0.7 all-gather.5.cloned.1.call-update
  8.7 0.0 all-reduce.4.cloned.1.call-start
  8.7 21.9 %all-gather.3.cloned.1.call-done = bf16[1,3584,1024]{2,1,0:T(8,128)(2,1)} async-done(((bf16[1,1792,1024]{2,1,0:T(8,128)(2,1)}), bf16[1,3584,1024]{2,1,0:T(8,128)(2,1)}) %all-gather.3.cloned.1.call-update) | async-done | bytes 7340048 | tf_op jit(solution)/shard_map/all_gather | solution.py:19
  30.6 10.4 %fusion.13 = bf16[640,1024]{1,0:T(8,128)(2,1)} fusion(bf16[1,3584,1024]{2,1,0:T(8,128)(2,1)} %all-gather.3.cloned.1.call-done, bf16[1,640,3584]{2,1,0:T(8,128)(2,1)} %param.5), kind=kOutput, calls=%fused_computation.19 | convolution fusion | flops 4698275840 | bytes 13238272 | tf_op jit(solution)/shard_map/dot_general | solution.py:17
  41.0 0.0 all-reduce.6.cloned.1.call-start
  41.1 10.6 %all-gather.5.cloned.1.call-done = bf16[1024,1,3584]{2,0,1:T(8,128)(2,1)} async-done(((bf16[1024,1,1792]{2,0,1:T(8,128)(2,1)}), bf16[1024,1,3584]{2,0,1:T(8,128)(2,1)}) %all-gather.5.cloned.1.call-update) | async-done | bytes 7340048 | tf_op jit(solution)/shard_map/all_gather | solution.py:22
  51.6 49.8 %all-reduce.4.cloned.1.call-done = bf16[640,1024]{1,0:T(8,128)(2,1)} async-done(((bf16[640,1024]{1,0:T(8,128)(2,1)}), bf16[640,1024]{1,0:T(8,128)(2,1)}) %all-reduce.4.cloned.1.call-update) | async-done | bytes 1310736 | tf_op jit(solution)/shard_map/psum | solution.py:26
  101.5 10.6 %fusion.8 = bf16[640,3584]{1,0:T(8,128)(2,1)} fusion(bf16[1024,1,3584]{2,0,1:T(8,128)(2,1)} %all-gather.5.cloned.1.call-done, bf16[640,1024]{1,0:T(8,128)(2,1)} %all-reduce.4.cloned.1.call-done, f32[1024]{0:T(1024)S(1)} %copy-done.2), kind=kOutput, calls=%fused_computation.12 | convolution fusion | flops 4703191040 | bytes 13242368 | tf_op jit(solution)/shard_map/dot_general | solution.py:30
  112.1 0.0 all-reduce.8.cloned.1.call-start
  112.1 0.6 copy-done.1
  112.8 166.1 %all-reduce.6.cloned.1.call-done = bf16[640,3584]{1,0:T(8,128)(2,1)} async-done(((bf16[640,3584]{1,0:T(8,128)(2,1)}), bf16[640,3584]{1,0:T(8,128)(2,1)}) %all-reduce.6.cloned.1.call-update) | async-done | bytes 4587536 | tf_op jit(solution)/shard_map/psum | solution.py:31
  278.9 11.8 %fusion.18 = bf16[640,1024]{1,0:T(8,128)(2,1)} fusion(bf16[1024,1,3584]{2,0,1:T(8,128)(2,1)} %all-gather.5.cloned.1.call-done, bf16[640,3584]{1,0:T(8,128)(2,1)} %all-reduce.6.cloned.1.call-done, bf16[1,640,3584]{2,1,0:T(8,128)(2,1)} %param.5, f32[3584]{0:T(1024)S(1)} %reduce), kind=kOutput, calls=%fused_computation.20 | convolution fusion | flops 4709744640 | bytes 17840128 | tf_op jit(solution)/shard_map/dot_general | solution.py:33
  290.7 0.0 reduce-scatter.3.cloned.1.call-start
  290.8 2.9 multiply_reduce_fusion
  293.7 7.1 %psum.31 = f32[1024]{0:T(1024)S(1)} all-reduce(f32[1024]{0:T(1024)S(1)} %multiply_reduce_fusion), channel_id=1, replica_groups=mesh['layer'=2,'latent'=8,'tok'=2] {'layer','tok'}, use_global_device_ids=true, to_apply=%region_4.0 | all-reduce | flops 1024 | bytes 8192 | tf_op jit(solution)/shard_map/psum | solution.py:25
  300.8 34.9 %all-reduce.8.cloned.1.call-done = bf16[640,1024]{1,0:T(8,128)(2,1)} async-done(((bf16[640,1024]{1,0:T(8,128)(2,1)}), bf16[640,1024]{1,0:T(8,128)(2,1)}) %all-reduce.8.cloned.1.call-update) | async-done | bytes 1310736 | tf_op jit(solution)/shard_map/psum | solution.py:36
  335.7 10.7 %fusion.6 = bf16[3584,1024]{0,1:T(8,128)(2,1)} fusion(bf16[1,640,3584]{2,1,0:T(8,128)(2,1)} %param.5, bf16[640,1024]{1,0:T(8,128)(2,1)} %all-reduce.8.cloned.1.call-done, bf16[640,1024]{1,0:T(8,128)(2,1)S(1)} %copy-done, f32[1024]{0:T(1024)S(1)} %add_sqrt_fusion, f32[1024]{0:T(1024)S(1)} %copy-done.2), kind=kOutput, calls=%fused_computation.10 | convolution fusion | flops 4706533376 | bytes 14557184 | tf_op jit(solution)/shard_map/dot_general | solution.py:41
  346.4 0.0 reduce-scatter.5.cloned.1.call-start
  346.4 0.5 convert_reduce_fusion
  346.9 15.2 %fusion.7 = bf16[1024,1,3584]{2,0,1:T(8,128)(2,1)} fusion(f32[1024]{0:T(1024)S(1)} %add_sqrt_fusion, bf16[1024,1,3584]{2,0,1:T(8,128)(2,1)} %all-gather.5.cloned.1.call-done, f32[1024]{0:T(1024)S(1)} %convert_reduce_fusion, bf16[640,3584]{1,0:T(8,128)(2,1)} %all-reduce.6.cloned.1.call-done, bf16[1,640,3584]{2,1,0:T(8,128)(2,1)} %param.5, ...), kind=kOutput, calls=%fused_computation.11 | convolution fusion | flops 4734386176 | bytes 25192448 | tf_op jit(solution)/shard_map/dot_general | solution.py:51
  362.1 0.3 reduce-scatter.3.cloned.1.call-done
  362.4 5.9 %copy.7 = bf16[1,1792,1024]{2,1,0:T(8,128)(2,1)} copy(bf16[1,1792,1024]{1,2,0:T(8,128)(2,1)} %bitcast.32) | data formatting | bytes 7340032
  368.4 14.1 %reduce-scatter.5.cloned.1.call-done = bf16[1024,1,1792]{2,0,1:T(8,128)(2,1)} async-done(((bf16[1024,1,3584]{2,0,1:T(8,128)(2,1)}), bf16[1024,1,1792]{2,0,1:T(8,128)(2,1)}) %reduce-scatter.5.cloned.1.call-update) | async-done | bytes 3670032 | tf_op jit(solution)/shard_map/reduce_scatter | solution.py:56
  (14 shorter events, 0.2 us)
Async XLA Ops:
  7.2 23.4 %all-gather.3.cloned.1.call-start = ((), (), s32[]{:S(2)}) async-start(), calls=%async_computation.2 | async-start | bytes 11010048 | tf_op jit(solution)/shard_map/all_gather | solution.py:19
  7.9 43.7 %all-gather.5.cloned.1.call-start = ((), (), s32[]{:S(2)}) async-start(), calls=%async_computation.4 | async-start | bytes 11010048 | tf_op jit(solution)/shard_map/all_gather | solution.py:22
  8.6 92.8 %copy-start.2 = (f32[1024]{0:T(1024)S(1)}, f32[1024]{0:T(1024)}, u32[]{:S(2)}) copy-start(f32[1024]{0:T(1024)} %param.7) | copy-start | bytes 12292
  8.7 92.8 %all-reduce.4.cloned.1.call-start = ((), (), s32[]{:S(2)}) async-start(), calls=%async_computation.3 | async-start | bytes 2621440 | tf_op jit(solution)/shard_map/psum | solution.py:26
  41.0 237.9 %all-reduce.6.cloned.1.call-start = ((), (), s32[]{:S(2)}) async-start(), calls=%async_computation.5 | async-start | bytes 9175040 | tf_op jit(solution)/shard_map/psum | solution.py:31
  112.1 0.7 copy-start.1
  112.1 223.6 %all-reduce.8.cloned.1.call-start = ((), (), s32[]{:S(2)}) async-start(), calls=%async_computation.6 | async-start | bytes 2621440 | tf_op jit(solution)/shard_map/psum | solution.py:36
  290.7 45.0 %copy-start = (bf16[640,1024]{1,0:T(8,128)(2,1)S(1)}, bf16[640,1024]{1,0:T(8,128)(2,1)}, u32[]{:S(2)}) copy-start(bf16[640,1024]{1,0:T(8,128)(2,1)} %all-reduce.4.cloned.1.call-done) | copy-start | bytes 3932164
  290.7 71.7 %reduce-scatter.3.cloned.1.call-start = ((), (), s32[]{:S(2)}) async-start(), calls=%async_computation.7 | async-start | bytes 11010048 | tf_op jit(solution)/shard_map/reduce_scatter | solution.py:40
  346.4 36.1 %reduce-scatter.5.cloned.1.call-start = ((), (), s32[]{:S(2)}) async-start(), calls=%async_computation.8 | async-start | bytes 11010048 | tf_op jit(solution)/shard_map/reduce_scatter | solution.py:56
Sparse Core Ops, SparseCore 0:
  9.5 20.9 all-gather.2
  32.1 19.4 all-gather.4
  54.5 46.9 all-reduce.3
  112.2 166.6 all-reduce.5
  290.8 44.7 all-reduce.7
  346.5 15.8 reduce-scatter.2
  365.4 17.0 reduce-scatter.4
where the time goes:
time: 390 us; the launch traced here: 389 us
  waiting for transfers between devices  299 us (77%)
  matrix products  58.7 us (15%)
  between operations  14.1 us (4%)
  blocking collectives  7.07 us (2%)
  local copies, waits for them, and re-layouts  6.58 us (2%)
    psum x1, waiting for transfers between devices, on_device(): lax.psum(partial_value.astype(jnp.bfloat16), 'latent').astype(jnp.float32)  166 us
    psum x1, waiting for transfers between devices, on_device(): preact = lax.psum(encoded.astype(jnp.bfloat16), 'layer').astype(jnp.float32)  49.8 us
    psum x1, waiting for transfers between devices, on_device(): lax.psum(back_part.astype(jnp.bfloat16), 'layer').astype(jnp.float32)  34.9 us
    all_gather x1, waiting for transfers between devices, on_device(): lax.all_gather(enc_weight, 'tok', axis=1, tiled=True)[0]  21.9 us
    dot_general x1, matrix products, on_device(): lax.dot_general(latents, recon_error, (((0,), (0,)), ((), ())), preferred...  15.2 us
    reduce_scatter x1, waiting for transfers between devices, on_device(): lax.psum_scatter(dec_part[:, None, :].astype(jnp.bfloat16), 'tok', scatte...  14.1 us
    dot_general x1, matrix products, on_device(): lax.dot_general(recon_error, dec_matrix, (((1,), (1,)), ((), ())), prefer...  11.8 us
    dot_general x1, matrix products, on_device(): lax.dot_general(columns, pre_grad, (((0,), (0,)), ((), ())), preferred_el...  10.7 us
  transfers between devices with their start and end apart: 7, of which 7 were waited for; matrix products, arithmetic and copies ran while one was open for 9% of the time, Pallas kernels for 0%

commit v1 on v0

v1 whole, which is shorter than its diff:
```python
import math

import jax
import jax.numpy as jnp
from jax import lax
from jax.sharding import PartitionSpec as P

LAMBDA = 1.0
EPSILON = 1e-06


def dot(a, b, dims):
    return lax.dot_general(a, b, (dims, ((), ())), preferred_element_type=jnp.float32)


def swap(x, axis):
    return lax.ppermute(x, axis, [(0, 1), (1, 0)])


def latent_sum(part):
    return lax.psum(part, "latent")


def on_device(activations, enc_weight, enc_bias, dec_weight, dec_bias):
    f32, bf16 = jnp.float32, jnp.bfloat16
    rows = activations[0]
    row_count = rows.shape[0]
    loss_scale = 1.0 / math.sqrt(row_count * lax.axis_size("tok"))
    enc, dec = enc_weight[0], dec_weight[:, 0, :]
    width = enc.shape[0]
    tok = lax.axis_index("tok")
    act_own = lax.dynamic_slice_in_dim(rows, tok * width, width, axis=1)
    act_sent = lax.dynamic_slice_in_dim(rows, (1 - tok) * width, width, axis=1)
    act_other = swap(act_sent, "tok")
    half_sq = jnp.sum(jnp.square(dec.astype(f32)), axis=1)
    dec_norms = jnp.sqrt(lax.psum(half_sq, ("layer", "tok")) + EPSILON)

    def token_terms(own, other):
        arrived = swap(other.astype(bf16), "tok")
        mine = (own + arrived.astype(f32)).astype(bf16)
        return mine.astype(f32) + swap(mine, "layer").astype(f32)

    pre_other = dot(act_other, enc, ((1,), (0,)))
    pre_own = dot(act_own, enc, ((1,), (0,)))
    preact = token_terms(pre_own, pre_other) + enc_bias
    positive = jnp.maximum(preact, 0.0)
    lat_own = (positive * positive).astype(bf16)
    lat_other = swap(lat_own, "tok")
    bias = lax.dynamic_slice_in_dim(dec_bias[0], tok * width, width, axis=0)

    def error(lat, act):
        part = dot(lat, dec, ((1,), (0,))).astype(bf16)
        return (latent_sum(part).astype(f32) + bias - act.astype(f32)).astype(bf16)

    err_own = error(lat_own, act_own)
    err_other = error(lat_other, act_other)
    back_other = dot(err_other, dec, ((1,), (1,)))
    back_own = dot(err_own, dec, ((1,), (1,)))
    back_proj = token_terms(back_own, back_other)
    grad_own = (loss_scale * (back_proj + LAMBDA * dec_norms) * 2.0 * positive).astype(bf16)
    grad_other = swap(grad_own, "tok")
    grad_enc = dot(act_own, grad_own, ((0,), (0,))) + dot(act_other, grad_other, ((0,), (0,)))
    col_totals = jnp.sum(lat_own.astype(f32), axis=0) + jnp.sum(lat_other.astype(f32), axis=0)
    grad_dec = loss_scale * (
        dot(lat_own, err_own, ((0,), (0,)))
        + dot(lat_other, err_other, ((0,), (0,)))
        + (LAMBDA * col_totals / dec_norms)[:, None] * dec.astype(f32)
    )
    return grad_enc.astype(bf16)[None], grad_dec.astype(bf16)[:, None, :]


def solution(mesh):
    placed = (
        P("layer", "tok", None),
        P("layer", "tok", "latent"),
        P("latent"),
        P("latent", "layer", "tok"),
        P("layer", None),
    )
    return jax.shard_map(
        on_device,
        mesh=mesh,
        in_specs=placed,
        out_specs=(P("layer", "tok", "latent"), P("latent", "layer", "tok")),
        check_vma=False,
    )
```

time: 390 us -> 310 us (0.79)
  waiting for transfers between devices: 299 us -> 202 us
  blocking collectives: 7.07 us -> 31.4 us
  matrix products: 58.7 us -> 45.5 us
  starting transfers between devices: 0.28 us -> 5.45 us
    psum x3 -> x1, waiting for transfers between devices: 251 us -> 169 us  [latent_sum(): return lax.psum(part, 'latent')]
    ppermute x0 -> x7, waiting for transfers between devices: none -> 33.4 us  [swap(): return lax.ppermute(x, axis, [(0, 1), (1, 0)])]
    all_gather x2 -> x0, waiting for transfers between devices: 32.4 us -> none  [the longest x1 21.9 us: on_device(): lax.all_gather(enc_weight, 'tok', axis=1, tiled=True)[0]]
    psum x1, blocking collectives: 7.07 us -> 31.4 us  [on_device(): dec_norms = jnp.sqrt(lax.psum(half_sq, ('layer', 'tok')) + EPSILON)]
    reduce_scatter x2 -> x0, waiting for transfers between devices: 14.4 us -> none  [the longest x1 14.1 us: on_device(): lax.psum_scatter(dec_part[:, None, :].astype(jnp.bfloat16), 'tok', scatte...]
    dot_general x5 -> x10, matrix products: 58.7 us -> 45.5 us  [dot(): lax.dot_general(a, b, (dims, ((), ())), preferred_element_type=jnp.float32)]
    ppermute x0 -> x7, starting transfers between devices: none -> 5.41 us  [swap(): return lax.ppermute(x, axis, [(0, 1), (1, 0)])]
    unnamed x7 -> x40, local copies, waits for them, and re-layouts: 6.58 us -> 2.4 us
  transfers between devices with their start and end apart: 7 -> 8, of which waited for: 7 -> 4; matrix products, arithmetic and copies ran while one was open for 9% -> 10% of each run, Pallas kernels for 0% -> 0%
where the time goes in v1:
time: 310 us
  waiting for transfers between devices  202 us (65%)
  matrix products  45.5 us (15%)
  blocking collectives  31.4 us (10%)
  between operations  14.4 us (5%)
  other arithmetic  6.79 us (2%)
  starting transfers between devices  5.45 us (2%)
  local copies, waits for them, and re-layouts  4.38 us (1%)
    psum x1, waiting for transfers between devices, latent_sum(): return lax.psum(part, 'latent')  169 us
    dot_general x10, matrix products, dot(): lax.dot_general(a, b, (dims, ((), ())), preferred_element_type=jnp.float32)  45.5 us
    ppermute x7, waiting for transfers between devices, swap(): return lax.ppermute(x, axis, [(0, 1), (1, 0)])  33.4 us
    psum x1, blocking collectives, on_device(): dec_norms = jnp.sqrt(lax.psum(half_sq, ('layer', 'tok')) + EPSILON)  31.4 us
  transfers between devices with their start and end apart: 8, of which 4 were waited for; matrix products, arithmetic and copies ran while one was open for 10% of the time, Pallas kernels for 0%

profile of v1, /device:TPU:0, one launch (start us, length us, event | category | flops | bytes accessed | tf_op | source)
XLA Modules:
  0.0 310.1 jit_solution(8151902796684183243)
XLA Ops:
  7.2 1.9 dynamic-slice_bitcast_fusion
  9.2 0.5 collective-permute-start
  9.7 4.1 %collective-permute-done = bf16[640,1792]{1,0:T(8,128)(2,1)S(1)} collective-permute-done((bf16[640,1792]{1,0:T(8,128)(2,1)S(1)}, bf16[640,1792]{1,0:T(8,128)(2,1)S(1)}, u32[]{:S(2)}, u32[]{:S(2)}) %collective-permute-start) | collective-permute-done | bytes 2293792 | tf_op jit(solution)/shard_map/ppermute | solution.py:17
  13.8 2.5 fusion.29
  16.8 5.3 %fusion.15 = f32[640,1024]{1,0:T(8,128)S(1)} fusion(bf16[1,1792,1024]{2,1,0:T(8,128)(2,1)} %param.6, bf16[1,640,3584]{2,1,0:T(8,128)(2,1)} %param.5, s32[]{:T(128)S(6)} %select_n.7), kind=kOutput, calls=%fused_computation.20 | convolution fusion | flops 2348810240 | bytes 8585220 | tf_op jit(solution)/shard_map/dot_general | solution.py:13
  22.6 2.7 collective-permute-start.2
  25.3 29.3 %collective-permute-done.2 = bf16[640,1024]{1,0:T(8,128)(2,1)S(1)} collective-permute-done((bf16[640,1024]{1,0:T(8,128)(2,1)S(1)}, bf16[640,1024]{1,0:T(8,128)(2,1)S(1)}, u32[]{:S(2)}, u32[]{:S(2)}) %collective-permute-start.2) | collective-permute-done | bytes 1310752 | tf_op jit(solution)/shard_map/ppermute | solution.py:17
  54.6 1.1 copy-done.2
  55.7 0.7 convert_reduce_fusion.1
  56.5 3.9 %fusion.18 = bf16[640,1792]{1,0:T(8,128)(2,1)} fusion(bf16[640,1024]{1,0:T(8,128)(2,1)S(1)} %get-tuple-element.5, bf16[1024,1,1792]{2,0,1:T(8,128)(2,1)S(1)} %copy-done.4), kind=kOutput, calls=%fused_computation.23 | convolution fusion | flops 2349957120 | bytes 7274496 | tf_op jit(solution)/shard_map/dot_general | solution.py:13
  60.4 1.1 copy-done.7
  61.5 3.9 %fusion.21 = bf16[640,1792]{1,0:T(8,128)(2,1)} fusion(bf16[640,1024]{1,0:T(8,128)(2,1)S(1)} %collective-permute-done.3, bf16[1024,1,1792]{2,0,1:T(8,128)(2,1)S(1)} %copy-done.4), kind=kOutput, calls=%fused_computation.24 | convolution fusion | flops 2349957120 | bytes 7274496 | tf_op jit(solution)/shard_map/dot_general | solution.py:13
  65.5 168.8 %all-reduce.3.cloned.1.call-done = (bf16[640,1792]{1,0:T(8,128)(2,1)}, bf16[640,1792]{1,0:T(8,128)(2,1)}) async-done(((bf16[640,1792]{1,0:T(8,128)(2,1)}, bf16[640,1792]{1,0:T(8,128)(2,1)}), (bf16[640,1792]{1,0:T(8,128)(2,1)}, bf16[640,1792]{1,0:T(8,128)(2,1)})) %all-reduce.3.cloned.1.call-update) | async-done | bytes 4587536 | tf_op jit(solution)/shard_map/psum | solution.py:21
  234.3 6.1 %fusion.32 = bf16[640,1024]{1,0:T(8,128)(2,1)S(1)} fusion(bf16[1024,1,1792]{2,0,1:T(8,128)(2,1)} %param.8, bf16[640,1792]{1,0:T(8,128)(2,1)} %copy-done.12, bf16[640,1792]{1,0:T(8,128)(2,1)} %get-tuple-element.3, f32[1792]{0:T(1024)S(1)} %dynamic-slice_reduce_fusion), kind=kOutput, calls=%fused_computation.39 | convolution fusion | flops 2355200000 | bytes 9575424 | tf_op jit(solution)/shard_map/dot_general | solution.py:13
  240.7 2.8 fusion.9
  244.0 1.5 collective-permute-start.5
  245.6 0.8 fusion
  246.4 31.4 %psum.23 = f32[1024]{0:T(1024)S(1)} all-reduce(f32[1024]{0:T(1024)S(1)} %fusion), channel_id=1, replica_groups=mesh['layer'=2,'latent'=8,'tok'=2] {'layer','tok'}, use_global_device_ids=true, to_apply=%region_3.0 | all-reduce | flops 1024 | bytes 8192 | tf_op jit(solution)/shard_map/psum | solution.py:36
  277.7 1.5 convert_reduce_fusion
  279.3 6.0 %fusion.35 = f32[1024,1792]{1,0:T(8,128)S(1)} fusion(bf16[640,1024]{1,0:T(8,128)(2,1)} %copy-done.7, bf16[640,1792]{1,0:T(8,128)(2,1)} %copy-done.12, bf16[640,1792]{1,0:T(8,128)(2,1)} %get-tuple-element.3, f32[1792]{0:T(1024)S(1)} %dynamic-slice_reduce_fusion), kind=kOutput, calls=%fused_computation.40 | convolution fusion | flops 2354544640 | bytes 13245440 | tf_op jit(solution)/shard_map/dot_general | solution.py:13
  285.4 2.8 multiply_convert_fusion
  288.3 7.2 %fusion.4 = bf16[1024,1,1792]{2,0,1:T(8,128)(2,1)} fusion(f32[1024,1792]{1,0:T(8,128)S(1)} %fusion.35, bf16[1024,1,1792]{2,0,1:T(8,128)(2,1)S(1)} %copy-done.6, f32[1024]{0:T(1024)S(1)} %get-tuple-element.6, bf16[640,1024]{1,0:T(8,128)(2,1)S(1)} %copy-done.9, bf16[640,1792]{1,0:T(8,128)(2,1)S(1)} %copy-done.15, f32[1792]{0:T(1024)S(1)} %dynamic-slice_reduce_fusion, ...), kind=kOutput, calls=%fused_computation.9 | convolution fusion | flops 2365554688 | bytes 20589572 | tf_op jit(solution)/shard_map/dot_general | solution.py:13
  295.5 3.1 fusion.24
  298.6 4.7 %fusion.17 = bf16[1,1792,1024]{2,1,0:T(8,128)(2,1)} fusion(f32[1792,1024]{1,0:T(8,128)S(1)} %fusion.24, bf16[640,1792]{1,0:T(8,128)(2,1)S(1)} %copy-done.13, bf16[640,1024]{1,0:T(8,128)(2,1)S(1)} %collective-permute-done.6), kind=kOutput, calls=%fused_computation.22 | convolution fusion | flops 2352480256 | bytes 14614528 | tf_op jit(solution)/shard_map/dot_general | solution.py:13
  (55 shorter events, 2.0 us)
Async XLA Ops:
  7.2 58.3 %copy-start = (f32[1,3584]{1,0:T(1,128)S(1)}, f32[1,3584]{1,0:T(1,128)}, u32[]{:S(2)}) copy-start(f32[1,3584]{1,0:T(1,128)} %param.9) | copy-start | bytes 43012
  7.2 227.1 %all-reduce.3.cloned.1.call-start = ((), (), s32[]{:S(2)}) async-start(), calls=%async_computation | async-start | bytes 9175040 | tf_op jit(solution)/shard_map/psum | solution.py:21
  7.2 6.6 %copy-start.11 = (bf16[1,1792,1024]{2,1,0:T(8,128)(2,1)S(1)}, bf16[1,1792,1024]{2,1,0:T(8,128)(2,1)}, u32[]{:S(2)}) copy-start(bf16[1,1792,1024]{2,1,0:T(8,128)(2,1)} %param.6) | copy-start | bytes 11010052
  9.2 4.6 %collective-permute-start = (bf16[640,1792]{1,0:T(8,128)(2,1)S(1)}, bf16[640,1792]{1,0:T(8,128)(2,1)S(1)}, u32[]{:S(2)}, u32[]{:S(2)}) collective-permute-start(bf16[640,1792]{1,0:T(8,128)(2,1)S(1)} %dynamic-slice_bitcast_fusion), channel_id=1, source_target_pairs={{0,1},{1,0},{2,3},{3,2},{4,5},{5,4},{6,7},{7,6},{8,9},{9,8},{10,11... | collective-permute-start | bytes 6881288 | tf_op jit(solution)/shard_map/ppermute | solution.py:17
  16.3 5.7 %collective-permute-start.1 = (bf16[640,1024]{1,0:T(8,128)(2,1)S(1)}, bf16[640,1024]{1,0:T(8,128)(2,1)S(1)}, u32[]{:S(2)}, u32[]{:S(2)}) collective-permute-start(bf16[640,1024]{1,0:T(8,128)(2,1)S(1)} %fusion.29), channel_id=1, source_target_pairs={{0,1},{1,0},{2,3},{3,2},{4,5},{5,4},{6,7},{7,6},{8,9},{9,8},{10,11... | collective-permute-start | bytes 3932168 | tf_op jit(solution)/shard_map/ppermute | solution.py:17
  22.0 33.7 %copy-start.10 = (f32[1024]{0:T(1024)S(1)}, f32[1024]{0:T(1024)}, u32[]{:S(2)}) copy-start(f32[1024]{0:T(1024)} %param.7) | copy-start | bytes 12292
  22.6 33.9 %copy-start.4 = (bf16[1024,1,1792]{2,0,1:T(8,128)(2,1)S(1)}, bf16[1024,1,1792]{2,0,1:T(8,128)(2,1)}, u32[]{:S(2)}) copy-start(bf16[1024,1,1792]{2,0,1:T(8,128)(2,1)} %param.8) | copy-start | bytes 11010052
  22.6 32.0 %collective-permute-start.2 = (bf16[640,1024]{1,0:T(8,128)(2,1)S(1)}, bf16[640,1024]{1,0:T(8,128)(2,1)S(1)}, u32[]{:S(2)}, u32[]{:S(2)}) collective-permute-start(bf16[640,1024]{1,0:T(8,128)(2,1)S(1)} %add_convert_fusion.2), channel_id=1, source_target_pairs={{0,16},{16,0},{1,17},{17,1},{2,18},{18,2},{3,19},{19,3},{4,20},{20... | collective-permute-start | bytes 3932168 | tf_op jit(solution)/shard_map/ppermute | solution.py:17
  56.4 4.0 %copy-start.8 = (bf16[640,1024]{1,0:T(8,128)(2,1)}, bf16[640,1024]{1,0:T(8,128)(2,1)S(1)}, u32[]{:S(2)}) copy-start(bf16[640,1024]{1,0:T(8,128)(2,1)S(1)} %get-tuple-element.5) | copy-start | bytes 3932164
  56.4 4.0 %collective-permute-start.3 = (bf16[640,1024]{1,0:T(8,128)(2,1)S(1)}, bf16[640,1024]{1,0:T(8,128)(2,1)S(1)}, u32[]{:S(2)}, u32[]{:S(2)}) collective-permute-start(bf16[640,1024]{1,0:T(8,128)(2,1)S(1)} %get-tuple-element.5), channel_id=1, source_target_pairs={{0,1},{1,0},{2,3},{3,2},{4,5},{5,4},{6,7},{7,6},{8,9},{9,8},{10,11... | collective-permute-start | bytes 3932168 | tf_op jit(solution)/shard_map/ppermute | solution.py:17
  65.4 175.1 %slice-start = ((s8[4587520]{0:T(1024)(128)(4,1)}), s8[393216]{0:T(1024)(128)(4,1)S(1)}, s32[]{:S(2)}) async-start(s8[4587520]{0:T(1024)(128)(4,1)} %bitcast.48), calls=%async_computation.1 | async-start | bytes 786432
  234.3 6.2 %copy-start.5 = (bf16[1024,1,1792]{2,0,1:T(8,128)(2,1)S(1)}, bf16[1024,1,1792]{2,0,1:T(8,128)(2,1)}, u32[]{:S(2)}) copy-start(bf16[1024,1,1792]{2,0,1:T(8,128)(2,1)} %param.8) | copy-start | bytes 11010052
  234.3 6.2 %slice-start.1 = ((s8[4587520]{0:T(1024)(128)(4,1)}), s8[4194304]{0:T(1024)(128)(4,1)S(1)}, s32[]{:S(2)}) async-start(s8[4587520]{0:T(1024)(128)(4,1)} %bitcast.48), calls=%async_computation.2 | async-start | bytes 8388608
  234.3 6.4 %copy-start.14 = (bf16[640,1792]{1,0:T(8,128)(2,1)S(1)}, bf16[640,1792]{1,0:T(8,128)(2,1)}, u32[]{:S(2)}) copy-start(bf16[640,1792]{1,0:T(8,128)(2,1)} %get-tuple-element.2) | copy-start | bytes 6881284
  240.4 3.1 collective-permute-start.4
  244.0 41.3 %collective-permute-start.5 = (bf16[640,1024]{1,0:T(8,128)(2,1)S(1)}, bf16[640,1024]{1,0:T(8,128)(2,1)}, u32[]{:S(2)}, u32[]{:S(2)}) collective-permute-start(bf16[640,1024]{1,0:T(8,128)(2,1)S(1)} %add_convert_fusion.1), channel_id=1, source_target_pairs={{0,16},{16,0},{1,17},{17,1},{2,18},{18,2},{3,19},{19,3},{4,20},{20... | collective-permute-start | bytes 3932168 | tf_op jit(solution)/shard_map/ppermute | solution.py:17
  279.3 6.0 %copy-start.3 = (bf16[640,1024]{1,0:T(8,128)(2,1)S(1)}, bf16[640,1024]{1,0:T(8,128)(2,1)}, u32[]{:S(2)}) copy-start(bf16[640,1024]{1,0:T(8,128)(2,1)} %copy-done.2) | copy-start | bytes 3932164
  279.3 8.9 %copy-start.15 = (bf16[640,1792]{1,0:T(8,128)(2,1)S(1)}, bf16[640,1792]{1,0:T(8,128)(2,1)}, u32[]{:S(2)}) copy-start(bf16[640,1792]{1,0:T(8,128)(2,1)} %get-tuple-element.2) | copy-start | bytes 6881284
  285.3 2.9 copy-start.6
  285.4 10.1 %slice-start.2 = ((s8[4587520]{0:T(1024)(128)(4,1)}), s8[4194304]{0:T(1024)(128)(4,1)S(1)}, s32[]{:S(2)}) async-start(s8[4587520]{0:T(1024)(128)(4,1)} %bitcast.50), calls=%async_computation.3 | async-start | bytes 8388608
  288.2 10.4 %collective-permute-start.6 = (bf16[640,1024]{1,0:T(8,128)(2,1)S(1)}, bf16[640,1024]{1,0:T(8,128)(2,1)S(1)}, u32[]{:S(2)}, u32[]{:S(2)}) collective-permute-start(bf16[640,1024]{1,0:T(8,128)(2,1)S(1)} %multiply_convert_fusion), channel_id=1, source_target_pairs={{0,1},{1,0},{2,3},{3,2},{4,5},{5,4},{6,7},{7,6},{8,9},{9,8},{10,11... | collective-permute-start | bytes 3932168 | tf_op jit(solution)/shard_map/ppermute | solution.py:17
  288.3 7.2 %slice-start.3 = ((s8[4587520]{0:T(1024)(128)(4,1)}), s8[393216]{0:T(1024)(128)(4,1)S(1)}, s32[]{:S(2)}) async-start(s8[4587520]{0:T(1024)(128)(4,1)} %bitcast.50), calls=%async_computation.4 | async-start | bytes 786432
  295.4 3.1 %copy-start.13 = (bf16[640,1792]{1,0:T(8,128)(2,1)S(1)}, bf16[640,1792]{1,0:T(8,128)(2,1)}, u32[]{:S(2)}) copy-start(bf16[640,1792]{1,0:T(8,128)(2,1)} %copy-done.12) | copy-start | bytes 6881284
  298.6 4.7 %copy-start.1 = (f32[1,3584]{1,0:T(1,128)S(1)}, f32[1,3584]{1,0:T(1,128)}, u32[]{:S(2)}) copy-start(f32[1,3584]{1,0:T(1,128)} %param.9) | copy-start | bytes 43012
  (4 other events, 7.6 us)
Sparse Core Ops, SparseCore 0:
  65.6 168.6 all-reduce.2

commit v2 on v1

--- a/solution.py
+++ b/solution.py
@@ -1,8 +1,11 @@
+import functools
 import math
 
 import jax
 import jax.numpy as jnp
 from jax import lax
+from jax.experimental import pallas as pl
+from jax.experimental.pallas import tpu as pltpu
 from jax.sharding import PartitionSpec as P
 
 LAMBDA = 1.0
@@ -17,8 +20,131 @@
     return lax.ppermute(x, axis, [(0, 1), (1, 0)])
 
 
-def latent_sum(part):
-    return lax.psum(part, "latent")
+def ring_kernel(
+    n, lat0, lat1, act0, act1, dec, bias, err0, err1, back0, back1,
+    slots, rs_send, rs_recv, ag_send, ag_recv,
+):
+    lats, acts, errs, backs = (lat0, lat1), (act0, act1), (err0, err1), (back0, back1)
+    half = n // 2
+    latent = lax.axis_index("latent")
+    odd = lax.rem(latent, 2)
+    place = lax.div(latent, 2) + odd * (n - 1 - 2 * lax.div(latent, 2))
+
+    def device_at(spot):
+        far = lax.div(spot, half)
+        return (1 - far) * 2 * spot + far * (2 * (n - 1 - spot) + 1)
+
+    right = device_at(lax.rem(place + 1, n))
+    left = device_at(lax.rem(place + n - 1, n))
+    targets = (right, left)
+
+    def chunk(way, step):
+        return lax.rem(place - step + 2 * n, n) if way == 0 else lax.rem(place + step + n, n)
+
+    def rs_copy(way, step):
+        return pltpu.make_async_remote_copy(
+            src_ref=slots.at[way, step],
+            dst_ref=slots.at[way, step + 1],
+            send_sem=rs_send.at[way, step],
+            recv_sem=rs_recv.at[way, step],
+            device_id={"latent": targets[way]},
+            device_id_type=pl.DeviceIdType.MESH,
+        )
+
+    def ag_copy(way, step, held):
+        return pltpu.make_async_remote_copy(
+            src_ref=errs[way].at[held],
+            dst_ref=errs[way].at[held],
+            send_sem=ag_send.at[way, step],
+            recv_sem=ag_recv.at[way, step],
+            device_id={"latent": targets[way]},
+            device_id_type=pl.DeviceIdType.MESH,
+        )
+
+    def partial(way, step):
+        return jnp.dot(lats[way][chunk(way, step)], dec[...], preferred_element_type=jnp.float32)
+
+    def project(way, held):
+        out = dot(errs[way][held], dec[...], ((1,), (1,)))
+        backs[way][held] = out.astype(backs[way].dtype)
+
+    barrier = pltpu.get_barrier_semaphore()
+    for target in targets:
+        pl.semaphore_signal(
+            barrier, inc=1, device_id={"latent": target}, device_id_type=pl.DeviceIdType.MESH
+        )
+    for way in range(2):
+        slots[way, 0] = partial(way, 0).astype(slots.dtype)
+    pl.semaphore_wait(barrier, 2)
+    for way in range(2):
+        rs_copy(way, 0).start()
+
+    @pl.loop(1, n - 1)
+    def _(step):
+        parts = [partial(way, step) for way in range(2)]
+        for way in range(2):
+            rs_copy(way, step - 1).wait_recv()
+            total = slots[way, step].astype(jnp.float32) + parts[way]
+            slots[way, step] = total.astype(slots.dtype)
+            rs_copy(way, step).start()
+
+    parts = [partial(way, n - 1) for way in range(2)]
+    for way in range(2):
+        held = chunk(way, n - 1)
+        rs_copy(way, n - 2).wait_recv()
+        total = slots[way, n - 1].astype(jnp.float32) + parts[way]
+        error = total + bias[...] - acts[way][held].astype(jnp.float32)
+        errs[way][held] = error.astype(errs[way].dtype)
+        ag_copy(way, 0, held).start()
+    for way in range(2):
+        project(way, chunk(way, n - 1))
+
+    @pl.loop(0, n - 2)
+    def _(step):
+        for way in range(2):
+            ag_copy(way, step, chunk(way, step)).wait_recv()
+            ag_copy(way, step + 1, chunk(way, step)).start()
+        for way in range(2):
+            project(way, chunk(way, step))
+
+    for way in range(2):
+        ag_copy(way, n - 2, chunk(way, n - 2)).wait_recv()
+    for way in range(2):
+        project(way, chunk(way, n - 2))
+
+    @pl.loop(0, n - 1)
+    def _(step):
+        for way in range(2):
+            rs_copy(way, step).wait_send()
+            ag_copy(way, step, chunk(way, step - 1 + n)).wait_send()
+
+
+def error_and_back(lat_own, lat_other, act_own, act_other, dec, bias):
+    n = lax.axis_size("latent")
+    rows, latents = lat_own.shape
+    width = dec.shape[1]
+    part = rows // n
+    cut = lambda x: x.reshape(n, part, x.shape[1])
+    shape = jax.ShapeDtypeStruct
+    errs = [shape((n, part, width), jnp.bfloat16)] * 2
+    backs = [shape((n, part, latents), jnp.float32), shape((n, part, latents), jnp.bfloat16)]
+    sems = pltpu.SemaphoreType.DMA((2, n - 1))
+    outs = pl.pallas_call(
+        functools.partial(ring_kernel, n),
+        out_shape=errs + backs,
+        in_specs=[pl.BlockSpec(memory_space=pltpu.VMEM)] * 6,
+        out_specs=[pl.BlockSpec(memory_space=pltpu.VMEM)] * 4,
+        scratch_shapes=[pltpu.VMEM((2, n, part, width), jnp.bfloat16), sems, sems, sems, sems],
+        compiler_params=pltpu.CompilerParams(
+            collective_id=0, has_side_effects=True, vmem_limit_bytes=48 * 2**20
+        ),
+        cost_estimate=pl.CostEstimate(
+            flops=8 * rows * latents * width,
+            bytes_accessed=2 * (latents * width + 4 * rows * width + 5 * rows * latents),
+            transcendentals=0,
+        ),
+    )(cut(lat_own), cut(lat_other), cut(act_own), cut(act_other), dec, bias[None])
+    return [x.reshape(rows, x.shape[2]) for x in outs]
 
 
 def on_device(activations, enc_weight, enc_bias, dec_weight, dec_bias):
@@ -48,14 +174,9 @@
     lat_other = swap(lat_own, "tok")
     bias = lax.dynamic_slice_in_dim(dec_bias[0], tok * width, width, axis=0)
 
-    def error(lat, act):
-        part = dot(lat, dec, ((1,), (0,))).astype(bf16)
-        return (latent_sum(part).astype(f32) + bias - act.astype(f32)).astype(bf16)
-
-    err_own = error(lat_own, act_own)
-    err_other = error(lat_other, act_other)
-    back_other = dot(err_other, dec, ((1,), (1,)))
-    back_own = dot(err_own, dec, ((1,), (1,)))
+    err_own, err_other, back_own, back_other = error_and_back(
+        lat_own, lat_other, act_own, act_other, dec, bias
+    )
     back_proj = token_terms(back_own, back_other)
     grad_own = (loss_scale * (back_proj + LAMBDA * dec_norms) * 2.0 * positive).astype(bf16)
     grad_other = swap(grad_own, "tok")

time: 310 us -> 227 us (0.73)
  waiting for transfers between devices: 202 us -> 39.3 us
  Pallas kernels: 0 us -> 115 us
  matrix products: 45.5 us -> 23.2 us
  between operations: 14.4 us -> 0.88 us
    psum x1 -> x0, waiting for transfers between devices: 169 us -> none  [latent_sum(): return lax.psum(part, 'latent')]
    pallas_call x0 -> x1, Pallas kernels: none -> 115 us  [error_and_back(): pl.pallas_call(functools.partial(ring_kernel, n), out_shape=errs + backs,...]
    dot_general x10 -> x6, matrix products: 45.5 us -> 23.2 us  [dot(): lax.dot_general(a, b, (dims, ((), ())), preferred_element_type=jnp.float32)]
    ppermute x7, waiting for transfers between devices: 33.4 us -> 39.3 us  [swap(): return lax.ppermute(x, axis, [(0, 1), (1, 0)])]
  transfers between devices with their start and end apart: 8 -> 7, of which waited for: 4 -> 5; matrix products, arithmetic and copies ran while one was open for 10% -> 7% of each run, Pallas kernels for 0% -> 0%
where the time goes in v2:
time: 227 us
  Pallas kernels  115 us (51%)
  waiting for transfers between devices  39.3 us (17%)
  blocking collectives  31.4 us (14%)
  matrix products  23.2 us (10%)
  other arithmetic  8.83 us (4%)
  starting transfers between devices  5.04 us (2%)
  local copies, waits for them, and re-layouts  3.15 us (1%)
    pallas_call x1, Pallas kernels, error_and_back(): pl.pallas_call(functools.partial(ring_kernel, n), out_shape=errs + backs,...  115 us
    ppermute x7, waiting for transfers between devices, swap(): return lax.ppermute(x, axis, [(0, 1), (1, 0)])  39.3 us
    psum x1, blocking collectives, on_device(): dec_norms = jnp.sqrt(lax.psum(half_sq, ('layer', 'tok')) + EPSILON)  31.4 us
    dot_general x6, matrix products, dot(): lax.dot_general(a, b, (dims, ((), ())), preferred_element_type=jnp.float32)  23.2 us
    ppermute x7, starting transfers between devices, swap(): return lax.ppermute(x, axis, [(0, 1), (1, 0)])  5.04 us
  transfers between devices with their start and end apart: 7, of which 5 were waited for; matrix products, arithmetic and copies ran while one was open for 7% of the time, Pallas kernels for 0%

profile of v2, /device:TPU:0, one launch (start us, length us, event | category | flops | bytes accessed | tf_op | source)
XLA Modules:
  0.0 226.8 jit_solution(2493475634940463186)
XLA Ops:
  0.7 2.8 %dynamic-slice_bitcast_fusion = (bf16[640,1792]{1,0:T(8,128)(2,1)S(1)}, bf16[1,640,1792]{2,1,0:T(8,128)(2,1)S(1)}) fusion(bf16[1,640,3584]{2,1,0:T(8,128)(2,1)} %param.5, s32[]{:T(128)S(6)} %select_n.8, s32[]{:T(128)S(6)} %select_n.7), kind=kLoop, calls=%fused_computation.24 | loop fusion | bytes 9175048 | tf_op jit(solution)/shard_map/dynamic_slice | solution.py:159
  3.5 0.5 collective-permute-start
  4.0 4.1 %collective-permute-done = bf16[640,1792]{1,0:T(8,128)(2,1)S(1)} collective-permute-done((bf16[640,1792]{1,0:T(8,128)(2,1)S(1)}, bf16[640,1792]{1,0:T(8,128)(2,1)S(1)}, u32[]{:S(2)}, u32[]{:S(2)}) %collective-permute-start) | collective-permute-done | bytes 2293792 | tf_op jit(solution)/shard_map/ppermute | solution.py:20
  8.1 2.6 %fusion.14 = bf16[640,1024]{1,0:T(8,128)(2,1)S(1)} fusion(bf16[640,1792]{1,0:T(8,128)(2,1)S(1)} %collective-permute-done, bf16[1,1792,1024]{2,1,0:T(8,128)(2,1)S(1)} %copy-done.10), kind=kOutput, calls=%fused_computation.25 | convolution fusion | flops 2349465600 | bytes 7274496 | tf_op jit(solution)/shard_map/dot_general | solution.py:16
  10.6 0.4 collective-permute-start.1
  11.1 2.5 %fusion.7 = f32[640,1024]{1,0:T(8,128)S(1)} fusion(bf16[1,1792,1024]{2,1,0:T(8,128)(2,1)S(1)} %copy-done.10, bf16[1,640,1792]{2,1,0:T(8,128)(2,1)S(1)} %get-tuple-element.13), kind=kOutput, calls=%fused_computation.10 | convolution fusion | flops 2348810240 | bytes 8585216 | tf_op jit(solution)/shard_map/dot_general | solution.py:16
  13.7 0.5 add_convert_fusion.1
  14.2 2.9 %collective-permute-start.2 = (bf16[640,1024]{1,0:T(8,128)(2,1)S(1)}, bf16[640,1024]{1,0:T(8,128)(2,1)S(1)}, u32[]{:S(2)}, u32[]{:S(2)}) collective-permute-start(bf16[640,1024]{1,0:T(8,128)(2,1)S(1)} %add_convert_fusion.1), channel_id=1, source_target_pairs={{0,16},{16,0},{1,17},{17,1},{2,18},{18,2},{3,19},{19,3},{4,20},{20... | collective-permute-start | bytes 3932168 | tf_op jit(solution)/shard_map/ppermute | solution.py:20
  17.2 29.1 %collective-permute-done.2 = bf16[640,1024]{1,0:T(8,128)(2,1)S(1)} collective-permute-done((bf16[640,1024]{1,0:T(8,128)(2,1)S(1)}, bf16[640,1024]{1,0:T(8,128)(2,1)S(1)}, u32[]{:S(2)}, u32[]{:S(2)}) %collective-permute-start.2) | collective-permute-done | bytes 1310752 | tf_op jit(solution)/shard_map/ppermute | solution.py:20
  46.3 0.7 convert_reduce_fusion.1
  47.1 3.0 %collective-permute-done.3 = bf16[640,1024]{1,0:T(8,128)(2,1)S(1)} collective-permute-done((bf16[640,1024]{1,0:T(8,128)(2,1)S(1)}, bf16[640,1024]{1,0:T(8,128)(2,1)S(1)}, u32[]{:S(2)}, u32[]{:S(2)}) %collective-permute-start.3) | collective-permute-done | bytes 1310752 | tf_op jit(solution)/shard_map/ppermute | solution.py:20
  50.1 115.0 %shard_map.68 = (bf16[8,80,1792]{2,1,0:T(8,128)(2,1)}, bf16[8,80,1792]{2,1,0:T(8,128)(2,1)}, f32[8,80,1024]{2,1,0:T(8,128)}, bf16[8,80,1024]{2,1,0:T(8,128)(2,1)S(1)}) custom-call(bf16[8,80,1024]{2,1,0:T(8,128)(2,1)S(1)} %bitcast.41, bf16[8,80,1024]{2,1,0:T(8,128)(2,1)S(1)} %bitcast.40, bf16[8,80,1792]{2,1,0:T(8,128)(2,1)} %bitcast.44, ...), custom_call_target="tpu_custom_call" | custom-call | flops 9395240960 | bytes 19398656 | tf_op jit(solution)/shard_map/pallas_call | solution.py:132
  165.1 3.0 %collective-permute-done.4 = bf16[640,1024]{1,0:T(8,128)(2,1)S(1)} collective-permute-done((bf16[640,1024]{1,0:T(8,128)(2,1)S(1)}, bf16[640,1024]{1,0:T(8,128)(2,1)S(1)}, u32[]{:S(2)}, u32[]{:S(2)}) %collective-permute-start.4) | collective-permute-done | bytes 1310752 | tf_op jit(solution)/shard_map/ppermute | solution.py:20
  168.2 3.5 %fusion.10 = bf16[640,1024]{1,0:T(8,128)(2,1)} fusion(f32[8,80,1024]{2,1,0:T(8,128)} %get-tuple-element.6, bf16[640,1024]{1,0:T(8,128)(2,1)S(1)} %collective-permute-done.4), kind=kLoop, calls=%fused_computation.14 | loop fusion | flops 1966080 | bytes 5242880 | tf_op jit(solution)/shard_map/convert_element_type | solution.py:166
  171.6 0.9 collective-permute-start.5
  172.6 0.8 fusion
  173.4 31.4 %psum.7 = f32[1024]{0:T(1024)S(1)} all-reduce(f32[1024]{0:T(1024)S(1)} %fusion), channel_id=1, replica_groups=mesh['layer'=2,'latent'=8,'tok'=2] {'layer','tok'}, use_global_device_ids=true, to_apply=%region_1.0 | all-reduce | flops 1024 | bytes 8192 | tf_op jit(solution)/shard_map/psum | solution.py:162
  204.8 0.2 convert_reduce_fusion
  205.0 5.0 %fusion.17 = f32[1024,1792]{1,0:T(8,128)S(1)} fusion(bf16[640,1024]{1,0:T(8,128)(2,1)S(1)} %collective-permute-done.3, bf16[640,1792]{1,0:T(8,128)(2,1)} %bitcast.47), kind=kOutput, calls=%fused_computation.30 | convolution fusion | flops 2348810240 | bytes 10944512 | tf_op jit(solution)/shard_map/dot_general | solution.py:16
  210.1 3.2 %multiply_convert_fusion = bf16[640,1024]{1,0:T(8,128)(2,1)S(1)} fusion(bf16[640,1024]{1,0:T(8,128)(2,1)} %collective-permute-done.5, bf16[640,1024]{1,0:T(8,128)(2,1)} %fusion.10, bf16[640,1024]{1,0:T(8,128)(2,1)S(1)} %copy-done.4, bf16[640,1024]{1,0:T(8,128)(2,1)S(1)} %copy-done.2, f32[1024]{0:T(1024)S(1)} %get-tuple-element.15, f32[1024]{0:T(1024)S(1)} %copy-done.9), kind=kLoop, calls=%fused_computation.17 | loop fusion | flops 7864320 | bytes 6561792 | tf_op jit(solution)/shard_map/convert_element_type | solution.py:181
  213.3 0.3 copy-done.13
  213.6 5.4 %fusion.4 = bf16[1024,1,1792]{2,0,1:T(8,128)(2,1)} fusion(f32[1024,1792]{1,0:T(8,128)S(1)} %fusion.17, f32[1024]{0:T(1024)S(1)} %get-tuple-element.14, bf16[1024,1,1792]{2,0,1:T(8,128)(2,1)S(1)} %copy-done.6, bf16[640,1024]{1,0:T(8,128)(2,1)S(1)} %get-tuple-element.11, bf16[640,1792]{1,0:T(8,128)(2,1)S(1)} %bitcast.46), kind=kOutput, calls=%fused_computation.7 | convolution fusion | flops 2359820288 | bytes 18288640 | tf_op jit(solution)/shard_map/dot_general | solution.py:16
  219.0 3.1 %fusion.11 = f32[1792,1024]{1,0:T(8,128)S(1)} fusion(bf16[640,1024]{1,0:T(8,128)(2,1)S(1)} %multiply_convert_fusion, bf16[1,640,1792]{2,1,0:T(8,128)(2,1)S(1)} %copy-done.8), kind=kOutput, calls=%fused_computation.21 | convolution fusion | flops 2348810240 | bytes 10944512 | tf_op jit(solution)/shard_map/dot_general | solution.py:16
  222.1 4.7 %fusion.9 = bf16[1,1792,1024]{2,1,0:T(8,128)(2,1)} fusion(f32[1792,1024]{1,0:T(8,128)S(1)} %fusion.11, bf16[640,1792]{1,0:T(8,128)(2,1)S(1)} %copy-done.12, bf16[640,1024]{1,0:T(8,128)(2,1)S(1)} %collective-permute-done.6), kind=kOutput, calls=%fused_computation.12 | convolution fusion | flops 2352480256 | bytes 14614528 | tf_op jit(solution)/shard_map/dot_general | solution.py:16
  (35 shorter events, 0.4 us)
Async XLA Ops:
  0.6 46.4 %copy-start = (f32[1,3584]{1,0:T(1,128)S(1)}, f32[1,3584]{1,0:T(1,128)}, u32[]{:S(2)}) copy-start(f32[1,3584]{1,0:T(1,128)} %param.9) | copy-start | bytes 43012
  0.7 7.4 %copy-start.10 = (bf16[1,1792,1024]{2,1,0:T(8,128)(2,1)S(1)}, bf16[1,1792,1024]{2,1,0:T(8,128)(2,1)}, u32[]{:S(2)}) copy-start(bf16[1,1792,1024]{2,1,0:T(8,128)(2,1)} %param.6) | copy-start | bytes 11010052
  3.5 7.6 %copy-start.7 = (bf16[1,640,1792]{2,1,0:T(8,128)(2,1)}, bf16[1,640,1792]{2,1,0:T(8,128)(2,1)S(1)}, u32[]{:S(2)}) copy-start(bf16[1,640,1792]{2,1,0:T(8,128)(2,1)S(1)} %get-tuple-element.13) | copy-start | bytes 6881284
  3.5 4.6 %collective-permute-start = (bf16[640,1792]{1,0:T(8,128)(2,1)S(1)}, bf16[640,1792]{1,0:T(8,128)(2,1)S(1)}, u32[]{:S(2)}, u32[]{:S(2)}) collective-permute-start(bf16[640,1792]{1,0:T(8,128)(2,1)S(1)} %get-tuple-element.12), channel_id=1, source_target_pairs={{0,1},{1,0},{2,3},{3,2},{4,5},{5,4},{6,7},{7,6},{8,9},{9,8},{10,11... | collective-permute-start | bytes 6881288 | tf_op jit(solution)/shard_map/ppermute | solution.py:20
  8.1 2.6 %copy-start.11 = (bf16[640,1792]{1,0:T(8,128)(2,1)}, bf16[640,1792]{1,0:T(8,128)(2,1)S(1)}, u32[]{:S(2)}) copy-start(bf16[640,1792]{1,0:T(8,128)(2,1)S(1)} %collective-permute-done) | copy-start | bytes 6881284
  10.6 3.1 %collective-permute-start.1 = (bf16[640,1024]{1,0:T(8,128)(2,1)S(1)}, bf16[640,1024]{1,0:T(8,128)(2,1)S(1)}, u32[]{:S(2)}, u32[]{:S(2)}) collective-permute-start(bf16[640,1024]{1,0:T(8,128)(2,1)S(1)} %fusion.14), channel_id=1, source_target_pairs={{0,1},{1,0},{2,3},{3,2},{4,5},{5,4},{6,7},{7,6},{8,9},{9,8},{10,11... | collective-permute-start | bytes 3932168 | tf_op jit(solution)/shard_map/ppermute | solution.py:20
  13.6 32.6 %copy-start.9 = (f32[1024]{0:T(1024)S(1)}, f32[1024]{0:T(1024)}, u32[]{:S(2)}) copy-start(f32[1024]{0:T(1024)} %param.7) | copy-start | bytes 12292
  14.2 32.7 %copy-start.1 = (bf16[640,1024]{1,0:T(8,128)(2,1)}, bf16[640,1024]{1,0:T(8,128)(2,1)S(1)}, u32[]{:S(2)}) copy-start(bf16[640,1024]{1,0:T(8,128)(2,1)S(1)} %add_convert_fusion.1) | copy-start | bytes 3932164
  14.2 32.0 %collective-permute-start.2 = (bf16[640,1024]{1,0:T(8,128)(2,1)S(1)}, bf16[640,1024]{1,0:T(8,128)(2,1)S(1)}, u32[]{:S(2)}, u32[]{:S(2)}) collective-permute-start(bf16[640,1024]{1,0:T(8,128)(2,1)S(1)} %add_convert_fusion.1), channel_id=1, source_target_pairs={{0,16},{16,0},{1,17},{17,1},{2,18},{18,2},{3,19},{19,3},{4,20},{20... | collective-permute-start | bytes 3932168 | tf_op jit(solution)/shard_map/ppermute | solution.py:20
  46.2 3.8 %copy-start.3 = (bf16[640,1024]{1,0:T(8,128)(2,1)}, bf16[640,1024]{1,0:T(8,128)(2,1)S(1)}, u32[]{:S(2)}) copy-start(bf16[640,1024]{1,0:T(8,128)(2,1)S(1)} %collective-permute-done.2) | copy-start | bytes 3932164
  47.0 3.1 %collective-permute-start.3 = (bf16[640,1024]{1,0:T(8,128)(2,1)S(1)}, bf16[640,1024]{1,0:T(8,128)(2,1)S(1)}, u32[]{:S(2)}, u32[]{:S(2)}) collective-permute-start(bf16[640,1024]{1,0:T(8,128)(2,1)S(1)} %get-tuple-element.11), channel_id=1, source_target_pairs={{0,1},{1,0},{2,3},{3,2},{4,5},{5,4},{6,7},{7,6},{8,9},{9,8},{10,11... | collective-permute-start | bytes 3932168 | tf_op jit(solution)/shard_map/ppermute | solution.py:20
  165.1 3.1 %collective-permute-start.4 = (bf16[640,1024]{1,0:T(8,128)(2,1)S(1)}, bf16[640,1024]{1,0:T(8,128)(2,1)S(1)}, u32[]{:S(2)}, u32[]{:S(2)}) collective-permute-start(bf16[640,1024]{1,0:T(8,128)(2,1)S(1)} %bitcast.42), channel_id=1, source_target_pairs={{0,1},{1,0},{2,3},{3,2},{4,5},{5,4},{6,7},{7,6},{8,9},{9,8},{10,11... | collective-permute-start | bytes 3932168 | tf_op jit(solution)/shard_map/ppermute | solution.py:20
  168.2 4.4 %copy-start.5 = (bf16[1024,1,1792]{2,0,1:T(8,128)(2,1)S(1)}, bf16[1024,1,1792]{2,0,1:T(8,128)(2,1)}, u32[]{:S(2)}) copy-start(bf16[1024,1,1792]{2,0,1:T(8,128)(2,1)} %param.8) | copy-start | bytes 11010052
  171.6 38.4 %collective-permute-start.5 = (bf16[640,1024]{1,0:T(8,128)(2,1)}, bf16[640,1024]{1,0:T(8,128)(2,1)}, u32[]{:S(2)}, u32[]{:S(2)}) collective-permute-start(bf16[640,1024]{1,0:T(8,128)(2,1)} %fusion.10), channel_id=1, source_target_pairs={{0,16},{16,0},{1,17},{17,1},{2,18},{18,2},{3,19},{19,3},{4,20},{20... | collective-permute-start | bytes 3932168 | tf_op jit(solution)/shard_map/ppermute | solution.py:20
  205.0 5.0 %copy-start.2 = (bf16[640,1024]{1,0:T(8,128)(2,1)S(1)}, bf16[640,1024]{1,0:T(8,128)(2,1)}, u32[]{:S(2)}) copy-start(bf16[640,1024]{1,0:T(8,128)(2,1)} %copy-done.1) | copy-start | bytes 3932164
  205.0 5.0 %copy-start.4 = (bf16[640,1024]{1,0:T(8,128)(2,1)S(1)}, bf16[640,1024]{1,0:T(8,128)(2,1)}, u32[]{:S(2)}) copy-start(bf16[640,1024]{1,0:T(8,128)(2,1)} %copy-done.3) | copy-start | bytes 3932164
  210.0 3.3 %copy-start.6 = (bf16[1024,1,1792]{2,0,1:T(8,128)(2,1)S(1)}, bf16[1024,1,1792]{2,0,1:T(8,128)(2,1)}, u32[]{:S(2)}) copy-start(bf16[1024,1,1792]{2,0,1:T(8,128)(2,1)} %param.8) | copy-start | bytes 11010052
  210.1 3.5 %copy-start.13 = (bf16[8,80,1792]{2,1,0:T(8,128)(2,1)S(1)}, bf16[8,80,1792]{2,1,0:T(8,128)(2,1)}, u32[]{:S(2)}) copy-start(bf16[8,80,1792]{2,1,0:T(8,128)(2,1)} %get-tuple-element.8) | copy-start | bytes 6881284
  213.2 8.9 %collective-permute-start.6 = (bf16[640,1024]{1,0:T(8,128)(2,1)S(1)}, bf16[640,1024]{1,0:T(8,128)(2,1)S(1)}, u32[]{:S(2)}, u32[]{:S(2)}) collective-permute-start(bf16[640,1024]{1,0:T(8,128)(2,1)S(1)} %multiply_convert_fusion), channel_id=1, source_target_pairs={{0,1},{1,0},{2,3},{3,2},{4,5},{5,4},{6,7},{7,6},{8,9},{9,8},{10,11... | collective-permute-start | bytes 3932168 | tf_op jit(solution)/shard_map/ppermute | solution.py:20
  213.6 5.4 %copy-start.8 = (bf16[1,640,1792]{2,1,0:T(8,128)(2,1)S(1)}, bf16[1,640,1792]{2,1,0:T(8,128)(2,1)}, u32[]{:S(2)}) copy-start(bf16[1,640,1792]{2,1,0:T(8,128)(2,1)} %copy-done.7) | copy-start | bytes 6881284
  219.0 3.1 %copy-start.12 = (bf16[640,1792]{1,0:T(8,128)(2,1)S(1)}, bf16[640,1792]{1,0:T(8,128)(2,1)}, u32[]{:S(2)}) copy-start(bf16[640,1792]{1,0:T(8,128)(2,1)} %copy-done.11) | copy-start | bytes 6881284

commit v3 on v2

v3 whole, which is shorter than its diff:
```python
import functools
import math

import jax
import jax.numpy as jnp
from jax import lax
from jax.experimental import pallas as pl
from jax.experimental.pallas import tpu as pltpu
from jax.sharding import PartitionSpec as P

LAMBDA = 1.0
EPSILON = 1e-06


def dot(a, b, dims):
    return lax.dot_general(a, b, (dims, ((), ())), preferred_element_type=jnp.float32)


def swap(x, axis):
    return lax.ppermute(x, axis, [(0, 1), (1, 0)])


def ring_kernel(
    n, pre, enc_bias, act0, act1, dec, bias,
    pre_in, lat0, lat1, err0, err1, back, back_in,
    slots, tok_out, tok_in, rs_send, rs_recv, ag_send, ag_recv, send_sems, recv_sems,
):
    lats, acts, errs = (lat0, lat1), (act0, act1), (err0, err1)
    half = n // 2
    latent, tok, layer = (lax.axis_index(name) for name in ("latent", "tok", "layer"))
    odd = lax.rem(latent, 2)
    place = lax.div(latent, 2) + odd * (n - 1 - 2 * lax.div(latent, 2))
    signs = (1 - 2 * tok, 2 * tok - 1)

    def device_at(spot):
        far = lax.div(spot, half)
        return (1 - far) * 2 * spot + far * (2 * (n - 1 - spot) + 1)

    targets = [{"latent": device_at(lax.rem(place + sign + n, n))} for sign in signs]
    core, other_layer = {"tok": 1 - tok}, {"layer": 1 - layer}

    def chunk(way, step):
        return lax.rem(place - signs[way] * step + 2 * n, n)

    def copy(src, dst, send, recv, device):
        return pltpu.make_async_remote_copy(
            src_ref=src, dst_ref=dst, send_sem=send, recv_sem=recv,
            device_id=device, device_id_type=pl.DeviceIdType.MESH,
        )

    def rs_copy(way, step):
        return copy(
            slots.at[way, step], slots.at[way, step + 1],
            rs_send.at[way, step], rs_recv.at[way, step], targets[way],
        )

    def ag_copy(way, step, held):
        return copy(
            errs[way].at[held], errs[way].at[held],
            ag_send.at[way, step], ag_recv.at[way, step], targets[way],
        )

    def swap_copy(kind, src, dst, step, device):
        return copy(src, dst, send_sems.at[kind, step], recv_sems.at[kind, step], device)

    def pre_copy(step):
        held = chunk(0, step)
        return swap_copy(0, pre.at[held], pre_in.at[held], step, other_layer)

    def lat_copy(step):
        held = chunk(0, step)
        return swap_copy(1, lat0.at[held], lat1.at[held], step, core)

    def lat_arrival(step):
        held = chunk(1, step)
        return swap_copy(1, lat0.at[held], lat1.at[held], step, core)

    def term_copy(step):
        return swap_copy(2, tok_out.at[step], tok_in.at[step], step, core)

    def back_copy(step, held):
        return swap_copy(3, back.at[held], back_in.at[held], step, other_layer)

    def encode(step):
        held = chunk(0, step)
        pre_copy(step).wait_recv()
        total = pre[held].astype(jnp.float32) + pre_in[held].astype(jnp.float32)
        positive = jnp.maximum(total + enc_bias[...], 0.0)
        lat0[held] = (positive * positive).astype(lat0.dtype)
        lat_copy(step).start()

    def partials(step):
        own = jnp.dot(lat0[chunk(0, step)], dec[...], preferred_element_type=jnp.float32)
        lat_arrival(step).wait_recv()
        other = jnp.dot(lat1[chunk(1, step)], dec[...], preferred_element_type=jnp.float32)
        return own, other

    def project(step, helds):
        other = dot(err1[helds[1]], dec[...], ((1,), (1,)))
        tok_out[step] = other.astype(tok_out.dtype)
        term_copy(step).start()
        own = dot(err0[helds[0]], dec[...], ((1,), (1,)))
        term_copy(step).wait_recv()
        back[helds[0]] = (own + tok_in[step].astype(jnp.float32)).astype(back.dtype)
        back_copy(step, helds[0]).start()

    barrier = pltpu.get_barrier_semaphore()
    for device in (*targets, core, other_layer):
        pl.semaphore_signal(
            barrier, inc=1, device_id=device, device_id_type=pl.DeviceIdType.MESH
        )
    pl.semaphore_wait(barrier, 4)

    @pl.loop(0, n)
    def _(step):
        pre_copy(step).start()

    encode(0)
    parts = partials(0)
    for way in range(2):
        slots[way, 0] = parts[way].astype(slots.dtype)
        rs_copy(way, 0).start()
    encode(1)

    @pl.loop(1, n - 1)
    def _(step):
        parts = partials(step)
        for way in range(2):
            rs_copy(way, step - 1).wait_recv()
            total = slots[way, step].astype(jnp.float32) + parts[way]
            slots[way, step] = total.astype(slots.dtype)
            rs_copy(way, step).start()
        encode(step + 1)

    parts = partials(n - 1)
    for way in range(2):
        held = chunk(way, n - 1)
        rs_copy(way, n - 2).wait_recv()
        total = slots[way, n - 1].astype(jnp.float32) + parts[way]
        error = total + bias[...] - acts[way][held].astype(jnp.float32)
        errs[way][held] = error.astype(errs[way].dtype)
        ag_copy(way, 0, held).start()
    project(0, [chunk(way, n - 1) for way in range(2)])

    @pl.loop(0, n - 1)
    def _(step):
        for way in range(2):
            ag_copy(way, step, chunk(way, step)).wait_recv()

            @pl.when(step < n - 2)
            def _():
                ag_copy(way, step + 1, chunk(way, step)).start()

        project(step + 1, [chunk(way, step) for way in range(2)])

    @pl.loop(0, n)
    def _(step):
        held = chunk(0, step - 1 + n)
        back_copy(step, held).wait_recv()
        back_copy(step, held).wait_send()
        term_copy(step).wait_send()
        pre_copy(step).wait_send()
        lat_copy(step).wait_send()

    @pl.loop(0, n - 1)
    def _(step):
        for way in range(2):
            rs_copy(way, step).wait_send()
            ag_copy(way, step, chunk(way, step - 1 + n)).wait_send()


def ring(pre, enc_bias, act_own, act_other, dec, bias):
    n = lax.axis_size("latent")
    rows, latents = pre.shape
    width = dec.shape[1]
    part = rows // n
    cut = lambda x: x.reshape(n, part, x.shape[1])
    narrow = jax.ShapeDtypeStruct((n, part, latents), jnp.bfloat16)
    wide = jax.ShapeDtypeStruct((n, part, width), jnp.bfloat16)
    ring_sems = pltpu.SemaphoreType.DMA((2, n - 1))
    swap_sems = pltpu.SemaphoreType.DMA((4, n))
    terms = pltpu.VMEM((n, part, latents), jnp.bfloat16)
    outs = pl.pallas_call(
        functools.partial(ring_kernel, n),
        out_shape=[narrow] * 3 + [wide] * 2 + [narrow] * 2,
        in_specs=[pl.BlockSpec(memory_space=pltpu.VMEM)] * 6,
        out_specs=[pl.BlockSpec(memory_space=pltpu.VMEM)] * 7,
        scratch_shapes=[pltpu.VMEM((2, n, part, width), jnp.bfloat16), terms, terms]
        + [ring_sems] * 4
        + [swap_sems] * 2,
        compiler_params=pltpu.CompilerParams(
            collective_id=0, has_side_effects=True, vmem_limit_bytes=48 * 2**20
        ),
        cost_estimate=pl.CostEstimate(
            flops=8 * rows * latents * width,
            bytes_accessed=2 * (latents * width + 4 * rows * width + 6 * rows * latents),
            transcendentals=0,
        ),
    )(cut(pre), enc_bias[None], cut(act_own), cut(act_other), dec, bias[None])
    return [x.reshape(rows, x.shape[2]) for x in outs]


def on_device(activations, enc_weight, enc_bias, dec_weight, dec_bias):
    f32, bf16 = jnp.float32, jnp.bfloat16
    rows = activations[0]
    row_count = rows.shape[0]
    loss_scale = 1.0 / math.sqrt(row_count * lax.axis_size("tok"))
    enc, dec = enc_weight[0], dec_weight[:, 0, :]
    width = enc.shape[0]
    tok = lax.axis_index("tok")
    act_own = lax.dynamic_slice_in_dim(rows, tok * width, width, axis=1)
    act_sent = lax.dynamic_slice_in_dim(rows, (1 - tok) * width, width, axis=1)
    act_other = swap(act_sent, "tok")
    half_sq = jnp.sum(jnp.square(dec.astype(f32)), axis=1)
    dec_norms = jnp.sqrt(lax.psum(half_sq, ("layer", "tok")) + EPSILON)

    pre_other = dot(act_other, enc, ((1,), (0,))).astype(bf16)
    pre_own = dot(act_own, enc, ((1,), (0,)))
    pre = (pre_own + swap(pre_other, "tok").astype(f32)).astype(bf16)
    bias = lax.dynamic_slice_in_dim(dec_bias[0], tok * width, width, axis=0)
    pre_in, lat_own, lat_other, err_own, err_other, back, back_in = ring(
        pre, enc_bias, act_own, act_other, dec, bias
    )
    positive = jnp.maximum(pre.astype(f32) + pre_in.astype(f32) + enc_bias, 0.0)
    back_proj = back.astype(f32) + back_in.astype(f32)
    grad_own = (loss_scale * (back_proj + LAMBDA * dec_norms) * 2.0 * positive).astype(bf16)
    grad_other = swap(grad_own, "tok")
    grad_enc = dot(act_own, grad_own, ((0,), (0,))) + dot(act_other, grad_other, ((0,), (0,)))
    col_totals = jnp.sum(lat_own.astype(f32), axis=0) + jnp.sum(lat_other.astype(f32), axis=0)
    grad_dec = loss_scale * (
        dot(lat_own, err_own, ((0,), (0,)))
        + dot(lat_other, err_other, ((0,), (0,)))
        + (LAMBDA * col_totals / dec_norms)[:, None] * dec.astype(f32)
    )
    return grad_enc.astype(bf16)[None], grad_dec.astype(bf16)[:, None, :]


def solution(mesh):
    placed = (
        P("layer", "tok", None),
        P("layer", "tok", "latent"),
        P("latent"),
        P("latent", "layer", "tok"),
        P("layer", None),
    )
    return jax.shard_map(
        on_device,
        mesh=mesh,
        in_specs=placed,
        out_specs=(P("layer", "tok", "latent"), P("latent", "layer", "tok")),
        check_vma=False,
    )
```

time: 227 us -> 179 us (0.79)
  waiting for transfers between devices: 39.3 us -> 4.07 us
  blocking collectives: 31.4 us -> 8.26 us
  Pallas kernels: 115 us -> 127 us
  starting transfers between devices: 5.04 us -> 1.46 us
  matrix products: 23.2 us -> 26.2 us
    ppermute x7 -> x3, waiting for transfers between devices: 39.3 us -> 4.07 us  [swap(): return lax.ppermute(x, axis, [(0, 1), (1, 0)])]
    psum x1, blocking collectives: 31.4 us -> 8.26 us  [on_device(): dec_norms = jnp.sqrt(lax.psum(half_sq, ('layer', 'tok')) + EPSILON)]
    pallas_call x1, Pallas kernels: 115 us -> 127 us  [ring(): pl.pallas_call(functools.partial(ring_kernel, n), out_shape=[narrow] * 3...]
    ppermute x7 -> x3, starting transfers between devices: 5.04 us -> 1.46 us  [swap(): return lax.ppermute(x, axis, [(0, 1), (1, 0)])]
    dot_general x6, matrix products: 23.2 us -> 26.2 us  [dot(): lax.dot_general(a, b, (dims, ((), ())), preferred_element_type=jnp.float32)]
  transfers between devices with their start and end apart: 7 -> 3, of which waited for: 5 -> 1; matrix products, arithmetic and copies ran while one was open for 7% -> 10% of each run, Pallas kernels for 0% -> 0%
where the time goes in v3:
time: 179 us
  Pallas kernels  127 us (71%)
  matrix products  26.2 us (15%)
  blocking collectives  8.26 us (5%)
  other arithmetic  6.92 us (4%)
  waiting for transfers between devices  4.07 us (2%)
  local copies, waits for them, and re-layouts  3.85 us (2%)
    pallas_call x1, Pallas kernels, ring(): pl.pallas_call(functools.partial(ring_kernel, n), out_shape=[narrow] * 3...  127 us
    dot_general x6, matrix products, dot(): lax.dot_general(a, b, (dims, ((), ())), preferred_element_type=jnp.float32)  26.2 us
    psum x1, blocking collectives, on_device(): dec_norms = jnp.sqrt(lax.psum(half_sq, ('layer', 'tok')) + EPSILON)  8.26 us
    ppermute x3, waiting for transfers between devices, swap(): return lax.ppermute(x, axis, [(0, 1), (1, 0)])  4.07 us
  transfers between devices with their start and end apart: 3, of which 1 were waited for; matrix products, arithmetic and copies ran while one was open for 10% of the time, Pallas kernels for 0%

profile of v3, /device:TPU:0, one launch (start us, length us, event | category | flops | bytes accessed | tf_op | source)
XLA Modules:
  0.0 179.0 jit_solution(10537942228845337564)
XLA Ops:
  0.6 0.0 copy-start
  0.6 0.0 copy-start.7
  0.7 2.8 %dynamic-slice_bitcast_fusion = (bf16[640,1792]{1,0:T(8,128)(2,1)S(1)}, bf16[1,640,1792]{2,1,0:T(8,128)(2,1)S(1)}) fusion(bf16[1,640,3584]{2,1,0:T(8,128)(2,1)} %param.5, s32[]{:T(128)S(6)} %select_n.8, s32[]{:T(128)S(6)} %select_n.7), kind=kLoop, calls=%fused_computation.28 | loop fusion | bytes 9175048 | tf_op jit(solution)/shard_map/dynamic_slice | solution.py:212
  3.5 0.0 copy-start.5
  3.5 0.5 collective-permute-start
  4.0 4.1 %collective-permute-done = bf16[640,1792]{1,0:T(8,128)(2,1)S(1)} collective-permute-done((bf16[640,1792]{1,0:T(8,128)(2,1)S(1)}, bf16[640,1792]{1,0:T(8,128)(2,1)S(1)}, u32[]{:S(2)}, u32[]{:S(2)}) %collective-permute-start) | collective-permute-done | bytes 2293792 | tf_op jit(solution)/shard_map/ppermute | solution.py:20
  8.1 3.6 %fusion.18 = bf16[640,1024]{1,0:T(8,128)(2,1)} fusion(bf16[640,1792]{1,0:T(8,128)(2,1)S(1)} %collective-permute-done, bf16[1,1792,1024]{2,1,0:T(8,128)(2,1)S(1)} %copy-done.7), kind=kOutput, calls=%fused_computation.29 | convolution fusion | flops 2349465600 | bytes 7274496 | tf_op jit(solution)/shard_map/dot_general | solution.py:16
  11.7 0.4 collective-permute-start.1
  12.1 0.8 fusion
  12.8 8.3 %psum.7 = f32[1024]{0:T(1024)S(1)} all-reduce(f32[1024]{0:T(1024)S(1)} %fusion), channel_id=1, replica_groups=mesh['layer'=2,'latent'=8,'tok'=2] {'layer','tok'}, use_global_device_ids=true, to_apply=%region_1.0 | all-reduce | flops 1024 | bytes 8192 | tf_op jit(solution)/shard_map/psum | solution.py:215
  21.1 4.6 %fusion.6 = f32[640,1024]{1,0:T(8,128)S(1)} fusion(bf16[1,1792,1024]{2,1,0:T(8,128)(2,1)} %param.6, bf16[1,640,1792]{2,1,0:T(8,128)(2,1)S(1)} %get-tuple-element.17), kind=kOutput, calls=%fused_computation.10 | convolution fusion | flops 2348810240 | bytes 8585216 | tf_op jit(solution)/shard_map/dot_general | solution.py:16
  25.7 0.0 copy-start.1
  25.7 2.9 %add_convert_fusion.1 = bf16[640,1024]{1,0:T(8,128)(2,1)} fusion(f32[640,1024]{1,0:T(8,128)S(1)} %fusion.6, bf16[640,1024]{1,0:T(8,128)(2,1)} %collective-permute-done.1), kind=kLoop, calls=%fused_computation.24 | loop fusion | flops 1966080 | bytes 5242880 | tf_op jit(solution)/shard_map/convert_element_type | solution.py:219
  28.7 127.4 %shard_map.68 = (bf16[8,80,1024]{2,1,0:T(8,128)(2,1)S(1)}, bf16[8,80,1024]{2,1,0:T(8,128)(2,1)S(1)}, bf16[8,80,1024]{2,1,0:T(8,128)(2,1)S(1)}, bf16[8,80,1792]{2...) custom-call(bf16[8,80,1024]{2,1,0:T(8,128)(2,1)} %bitcast.53, ...), custom_call_target="tpu_custom_call" | custom-call | flops 9395240960 | bytes 20709376 | tf_op jit(solution)/shard_map/pallas_call | solution.py:183
  156.1 1.8 %convert_add_fusion.1 = f32[8,80,1024]{2,1,0:T(8,128)S(1)} fusion(bf16[8,80,1024]{2,1,0:T(8,128)(2,1)} %get-tuple-element.10, bf16[8,80,1024]{2,1,0:T(8,128)(2,1)S(1)} %get-tuple-element.9), kind=kLoop, calls=%fused_computation.23 | loop fusion | flops 1966080 | bytes 5242880 | tf_op jit(solution)/shard_map/add | solution.py:225
  157.9 0.4 convert_reduce_fusion
  158.4 0.9 copy-done.2
  159.3 0.9 fusion.13
  160.2 0.6 collective-permute-start.2
  160.8 0.1 copy-done.10
  160.9 3.1 %fusion.21 = f32[1024,1792,1]{1,0,2:T(8,128)S(1)} fusion(bf16[8,80,1024]{2,1,0:T(8,128)(2,1)S(1)} %get-tuple-element.12, bf16[8,80,1792]{2,1,0:T(8,128)(2,1)S(1)} %copy-done.10), kind=kOutput, calls=%fused_computation.34 | convolution fusion | flops 2348810240 | bytes 10944512 | tf_op jit(solution)/shard_map/dot_general | solution.py:16
  164.1 3.1 %fusion.15 = f32[1792,1024]{1,0:T(8,128)S(1)} fusion(bf16[640,1024]{1,0:T(8,128)(2,1)S(1)} %fusion.13, bf16[1,640,1792]{2,1,0:T(8,128)(2,1)S(1)} %copy-done.6), kind=kOutput, calls=%fused_computation.25 | convolution fusion | flops 2348810240 | bytes 10944512 | tf_op jit(solution)/shard_map/dot_general | solution.py:16
  167.1 7.2 %fusion.9 = bf16[1024,1,1792]{2,0,1:T(8,128)(2,1)} fusion(f32[1024]{0:T(1024)S(1)} %get-tuple-element.18, bf16[8,80,1024]{2,1,0:T(8,128)(2,1)S(1)} %get-tuple-element.14, bf16[8,80,1792]{2,1,0:T(8,128)(2,1)} %get-tuple-element.15, f32[1024,1792,1]{1,0,2:T(8,128)S(1)} %fusion.21, bf16[1024,1,1792]{2,0,1:T(8,128)(2,1)S(1)} %copy-done.4), kind=kOutput, calls=%fused_computation.13 | convolution fusion | flops 2359820288 | bytes 18288640 | tf_op jit(solution)/shard_map/dot_general | solution.py:16
  174.3 4.7 %fusion.8 = bf16[1,1792,1024]{2,1,0:T(8,128)(2,1)} fusion(f32[1792,1024]{1,0:T(8,128)S(1)} %fusion.15, bf16[640,1792]{1,0:T(8,128)(2,1)S(1)} %copy-done.9, bf16[640,1024]{1,0:T(8,128)(2,1)S(1)} %collective-permute-done.2), kind=kOutput, calls=%fused_computation.12 | convolution fusion | flops 2352480256 | bytes 14614528 | tf_op jit(solution)/shard_map/dot_general | solution.py:16
  (20 shorter events, 0.1 us)
Async XLA Ops:
  0.6 20.5 %copy-start = (f32[1,3584]{1,0:T(1,128)S(1)}, f32[1,3584]{1,0:T(1,128)}, u32[]{:S(2)}) copy-start(f32[1,3584]{1,0:T(1,128)} %param.9) | copy-start | bytes 43012
  0.6 7.4 %copy-start.7 = (bf16[1,1792,1024]{2,1,0:T(8,128)(2,1)S(1)}, bf16[1,1792,1024]{2,1,0:T(8,128)(2,1)}, u32[]{:S(2)}) copy-start(bf16[1,1792,1024]{2,1,0:T(8,128)(2,1)} %param.6) | copy-start | bytes 11010052
  3.5 17.7 %copy-start.5 = (bf16[1,640,1792]{2,1,0:T(8,128)(2,1)}, bf16[1,640,1792]{2,1,0:T(8,128)(2,1)S(1)}, u32[]{:S(2)}) copy-start(bf16[1,640,1792]{2,1,0:T(8,128)(2,1)S(1)} %get-tuple-element.17) | copy-start | bytes 6881284
  3.5 8.6 %copy-start.3 = (bf16[1024,1,1792]{2,0,1:T(8,128)(2,1)S(1)}, bf16[1024,1,1792]{2,0,1:T(8,128)(2,1)}, u32[]{:S(2)}) copy-start(bf16[1024,1,1792]{2,0,1:T(8,128)(2,1)} %param.8) | copy-start | bytes 11010052
  3.5 4.6 %collective-permute-start = (bf16[640,1792]{1,0:T(8,128)(2,1)S(1)}, bf16[640,1792]{1,0:T(8,128)(2,1)S(1)}, u32[]{:S(2)}, u32[]{:S(2)}) collective-permute-start(bf16[640,1792]{1,0:T(8,128)(2,1)S(1)} %get-tuple-element.16), channel_id=1, source_target_pairs={{0,1},{1,0},{2,3},{3,2},{4,5},{5,4},{6,7},{7,6},{8,9},{9,8},{10,11... | collective-permute-start | bytes 6881288 | tf_op jit(solution)/shard_map/ppermute | solution.py:20
  8.1 3.6 %copy-start.8 = (bf16[640,1792]{1,0:T(8,128)(2,1)}, bf16[640,1792]{1,0:T(8,128)(2,1)S(1)}, u32[]{:S(2)}) copy-start(bf16[640,1792]{1,0:T(8,128)(2,1)S(1)} %collective-permute-done) | copy-start | bytes 6881284
  11.7 14.1 %collective-permute-start.1 = (bf16[640,1024]{1,0:T(8,128)(2,1)}, bf16[640,1024]{1,0:T(8,128)(2,1)}, u32[]{:S(2)}, u32[]{:S(2)}) collective-permute-start(bf16[640,1024]{1,0:T(8,128)(2,1)} %fusion.18), channel_id=1, source_target_pairs={{0,1},{1,0},{2,3},{3,2},{4,5},{5,4},{6,7},{7,6},{8,9},{9,8},{10,11... | collective-permute-start | bytes 3932168 | tf_op jit(solution)/shard_map/ppermute | solution.py:20
  25.7 3.0 %copy-start.1 = (f32[1024]{0:T(1024)S(1)}, f32[1024]{0:T(1024)}, u32[]{:S(2)}) copy-start(f32[1024]{0:T(1024)} %param.7) | copy-start | bytes 12292
  157.9 1.3 copy-start.2
  159.3 1.6 copy-start.10
  160.2 14.1 %collective-permute-start.2 = (bf16[640,1024]{1,0:T(8,128)(2,1)S(1)}, bf16[640,1024]{1,0:T(8,128)(2,1)S(1)}, u32[]{:S(2)}, u32[]{:S(2)}) collective-permute-start(bf16[640,1024]{1,0:T(8,128)(2,1)S(1)} %fusion.13), channel_id=1, source_target_pairs={{0,1},{1,0},{2,3},{3,2},{4,5},{5,4},{6,7},{7,6},{8,9},{9,8},{10,11... | collective-permute-start | bytes 3932168 | tf_op jit(solution)/shard_map/ppermute | solution.py:20
  160.9 3.1 %copy-start.6 = (bf16[1,640,1792]{2,1,0:T(8,128)(2,1)S(1)}, bf16[1,640,1792]{2,1,0:T(8,128)(2,1)}, u32[]{:S(2)}) copy-start(bf16[1,640,1792]{2,1,0:T(8,128)(2,1)} %copy-done.5) | copy-start | bytes 6881284
  164.0 3.1 %copy-start.4 = (bf16[1024,1,1792]{2,0,1:T(8,128)(2,1)S(1)}, bf16[1024,1,1792]{2,0,1:T(8,128)(2,1)}, u32[]{:S(2)}) copy-start(bf16[1024,1,1792]{2,0,1:T(8,128)(2,1)} %param.8) | copy-start | bytes 11010052
  167.1 7.2 %copy-start.9 = (bf16[640,1792]{1,0:T(8,128)(2,1)S(1)}, bf16[640,1792]{1,0:T(8,128)(2,1)}, u32[]{:S(2)}) copy-start(bf16[640,1792]{1,0:T(8,128)(2,1)} %copy-done.8) | copy-start | bytes 6881284

commit v4 on v3

--- a/solution.py
+++ b/solution.py
@@ -21,9 +21,9 @@
 
 
 def ring_kernel(
-    n, pre, enc_bias, act0, act1, dec, bias,
-    pre_in, lat0, lat1, err0, err1, back, back_in,
-    slots, tok_out, tok_in, rs_send, rs_recv, ag_send, ag_recv, send_sems, recv_sems,
+    n, pre, enc_bias, act0, act1, dec, bias, norm,
+    pre_in, lat0, lat1, err0, err1, back, back_in, norm_sum,
+    slots, tok_out, tok_in, norm_core, norm_chip, norm_in, rs_send, rs_recv, ag_send, ag_recv, send_sems, recv_sems,
 ):
     lats, acts, errs = (lat0, lat1), (act0, act1), (err0, err1)
     half = n // 2
@@ -80,6 +80,11 @@
 
     def back_copy(step, held):
         return swap_copy(3, back.at[held], back_in.at[held], step, other_layer)
+
+    def norm_copy(kind):
+        if kind == 4:
+            return swap_copy(4, norm, norm_core, 0, core)
+        return swap_copy(5, norm_chip, norm_in, 0, other_layer)
 
     def encode(step):
         held = chunk(0, step)
@@ -110,6 +115,7 @@
             barrier, inc=1, device_id=device, device_id_type=pl.DeviceIdType.MESH
         )
     pl.semaphore_wait(barrier, 4)
+    norm_copy(4).start()
 
     @pl.loop(0, n)
     def _(step):
@@ -121,6 +127,9 @@
         slots[way, 0] = parts[way].astype(slots.dtype)
         rs_copy(way, 0).start()
     encode(1)
+    norm_copy(4).wait_recv()
+    norm_chip[...] = norm[...] + norm_core[...]
+    norm_copy(5).start()
 
     @pl.loop(1, n - 1)
     def _(step):
@@ -141,6 +150,10 @@
         errs[way][held] = error.astype(errs[way].dtype)
         ag_copy(way, 0, held).start()
     project(0, [chunk(way, n - 1) for way in range(2)])
+    norm_copy(5).wait_recv()
+    norm_sum[...] = norm_chip[...] + norm_in[...]
+    norm_copy(4).wait_send()
+    norm_copy(5).wait_send()
 
     @pl.loop(0, n - 1)
     def _(step):
@@ -169,7 +182,7 @@
             ag_copy(way, step, chunk(way, step - 1 + n)).wait_send()
 
 
-def ring(pre, enc_bias, act_own, act_other, dec, bias):
+def ring(pre, enc_bias, act_own, act_other, dec, bias, norm):
     n = lax.axis_size("latent")
     rows, latents = pre.shape
     width = dec.shape[1]
@@ -178,14 +191,17 @@
     narrow = jax.ShapeDtypeStruct((n, part, latents), jnp.bfloat16)
     wide = jax.ShapeDtypeStruct((n, part, width), jnp.bfloat16)
     ring_sems = pltpu.SemaphoreType.DMA((2, n - 1))
-    swap_sems = pltpu.SemaphoreType.DMA((4, n))
+    swap_sems = pltpu.SemaphoreType.DMA((6, n))
+    norms = pltpu.VMEM((1, latents), jnp.float32)
     terms = pltpu.VMEM((n, part, latents), jnp.bfloat16)
     outs = pl.pallas_call(
         functools.partial(ring_kernel, n),
-        out_shape=[narrow] * 3 + [wide] * 2 + [narrow] * 2,
-        in_specs=[pl.BlockSpec(memory_space=pltpu.VMEM)] * 6,
-        out_specs=[pl.BlockSpec(memory_space=pltpu.VMEM)] * 7,
+        out_shape=[narrow] * 3 + [wide] * 2 + [narrow] * 2
+        + [jax.ShapeDtypeStruct((1, latents), jnp.float32)],
+        in_specs=[pl.BlockSpec(memory_space=pltpu.VMEM)] * 7,
+        out_specs=[pl.BlockSpec(memory_space=pltpu.VMEM)] * 8,
         scratch_shapes=[pltpu.VMEM((2, n, part, width), jnp.bfloat16), terms, terms]
+        + [norms] * 3
         + [ring_sems] * 4
         + [swap_sems] * 2,
         compiler_params=pltpu.CompilerParams(
@@ -196,8 +212,8 @@
             bytes_accessed=2 * (latents * width + 4 * rows * width + 6 * rows * latents),
             transcendentals=0,
         ),
-    )(cut(pre), enc_bias[None], cut(act_own), cut(act_other), dec, bias[None])
-    return [x.reshape(rows, x.shape[2]) for x in outs]
+    )(cut(pre), enc_bias[None], cut(act_own), cut(act_other), dec, bias[None], norm[None])
+    return [x.reshape(rows, x.shape[2]) for x in outs[:-1]] + [outs[-1][0]]
 
 
 def on_device(activations, enc_weight, enc_bias, dec_weight, dec_bias):
@@ -212,15 +228,15 @@
     act_sent = lax.dynamic_slice_in_dim(rows, (1 - tok) * width, width, axis=1)
     act_other = swap(act_sent, "tok")
     half_sq = jnp.sum(jnp.square(dec.astype(f32)), axis=1)
-    dec_norms = jnp.sqrt(lax.psum(half_sq, ("layer", "tok")) + EPSILON)
 
     pre_other = dot(act_other, enc, ((1,), (0,))).astype(bf16)
     pre_own = dot(act_own, enc, ((1,), (0,)))
     pre = (pre_own + swap(pre_other, "tok").astype(f32)).astype(bf16)
     bias = lax.dynamic_slice_in_dim(dec_bias[0], tok * width, width, axis=0)
-    pre_in, lat_own, lat_other, err_own, err_other, back, back_in = ring(
-        pre, enc_bias, act_own, act_other, dec, bias
-    )
+    pre_in, lat_own, lat_other, err_own, err_other, back, back_in, norm_sq = ring(
+        pre, enc_bias, act_own, act_other, dec, bias, half_sq
+    )
+    dec_norms = jnp.sqrt(norm_sq + EPSILON)
     positive = jnp.maximum(pre.astype(f32) + pre_in.astype(f32) + enc_bias, 0.0)
     back_proj = back.astype(f32) + back_in.astype(f32)
     grad_own = (loss_scale * (back_proj + LAMBDA * dec_norms) * 2.0 * positive).astype(bf16)

time: 179 us -> 170 us (0.950)
  blocking collectives: 8.26 us -> 0 us
  Pallas kernels: 127 us -> 131 us
  matrix products: 26.2 us -> 23.1 us
    psum x1 -> x0, blocking collectives: 8.26 us -> none  [on_device(): dec_norms = jnp.sqrt(lax.psum(half_sq, ('layer', 'tok')) + EPSILON)]
    pallas_call x1, Pallas kernels: 127 us -> 131 us  [ring(): pl.pallas_call(functools.partial(ring_kernel, n), out_shape=[narrow] * 3...]
    dot_general x6, matrix products: 26.2 us -> 23.1 us  [dot(): lax.dot_general(a, b, (dims, ((), ())), preferred_element_type=jnp.float32)]
where the time goes in v4:
time: 170 us
  Pallas kernels  131 us (77%)
  matrix products  23.1 us (14%)
  other arithmetic  5.69 us (3%)
  local copies, waits for them, and re-layouts  4.5 us (3%)
  waiting for transfers between devices  4.07 us (2%)
    pallas_call x1, Pallas kernels, ring(): pl.pallas_call(functools.partial(ring_kernel, n), out_shape=[narrow] * 3...  131 us
    dot_general x6, matrix products, dot(): lax.dot_general(a, b, (dims, ((), ())), preferred_element_type=jnp.float32)  23.1 us
    ppermute x3, waiting for transfers between devices, swap(): return lax.ppermute(x, axis, [(0, 1), (1, 0)])  4.07 us
  transfers between devices with their start and end apart: 3, of which 1 were waited for; matrix products, arithmetic and copies ran while one was open for 10% of the time, Pallas kernels for 0%

profile of v4, /device:TPU:0, one launch (start us, length us, event | category | flops | bytes accessed | tf_op | source)
XLA Modules:
  0.0 170.2 jit_solution(2717320481313911984)
XLA Ops:
  0.6 0.0 copy-start
  0.7 2.8 %dynamic-slice_bitcast_fusion = (bf16[640,1792]{1,0:T(8,128)(2,1)S(1)}, bf16[1,640,1792]{2,1,0:T(8,128)(2,1)S(1)}) fusion(bf16[1,640,3584]{2,1,0:T(8,128)(2,1)} %param.5, s32[]{:T(128)S(6)} %select_n.8, s32[]{:T(128)S(6)} %select_n.7), kind=kLoop, calls=%fused_computation.28 | loop fusion | bytes 9175048 | tf_op jit(solution)/shard_map/dynamic_slice | solution.py:228
  3.5 0.0 copy-start.5
  3.5 0.0 copy-start.3
  3.5 0.5 collective-permute-start
  4.0 4.1 %collective-permute-done = bf16[640,1792]{1,0:T(8,128)(2,1)S(1)} collective-permute-done((bf16[640,1792]{1,0:T(8,128)(2,1)S(1)}, bf16[640,1792]{1,0:T(8,128)(2,1)S(1)}, u32[]{:S(2)}, u32[]{:S(2)}) %collective-permute-start) | collective-permute-done | bytes 2293792 | tf_op jit(solution)/shard_map/ppermute | solution.py:20
  8.1 2.6 %fusion.18 = bf16[640,1024]{1,0:T(8,128)(2,1)S(1)} fusion(bf16[640,1792]{1,0:T(8,128)(2,1)S(1)} %collective-permute-done, bf16[1,1792,1024]{2,1,0:T(8,128)(2,1)S(1)} %copy-done.7), kind=kOutput, calls=%fused_computation.29 | convolution fusion | flops 2349465600 | bytes 7274496 | tf_op jit(solution)/shard_map/dot_general | solution.py:16
  10.6 0.4 collective-permute-start.1
  11.1 0.8 fusion
  11.9 2.5 %fusion.6 = f32[640,1024]{1,0:T(8,128)S(1)} fusion(bf16[1,1792,1024]{2,1,0:T(8,128)(2,1)S(1)} %copy-done.7, bf16[1,640,1792]{2,1,0:T(8,128)(2,1)S(1)} %get-tuple-element.19), kind=kOutput, calls=%fused_computation.10 | convolution fusion | flops 2348810240 | bytes 8585216 | tf_op jit(solution)/shard_map/dot_general | solution.py:16
  14.4 0.0 copy-start.1
  14.4 1.6 add_convert_fusion.1
  16.1 130.8 %shard_map.68 = (bf16[8,80,1024]{2,1,0:T(8,128)(2,1)S(1)}, bf16[8,80,1024]{2,1,0:T(8,128)(2,1)S(1)}, bf16[8,80,1024]{2,1,0:T(8,128)(2,1)S(1)}, bf16[8,80,1792]{2...) custom-call(bf16[8,80,1024]{2,1,0:T(8,128)(2,1)} %bitcast.57, ...), custom_call_target="tpu_custom_call" | custom-call | flops 9395240960 | bytes 20709376 | tf_op jit(solution)/shard_map/pallas_call | solution.py:197
  146.9 1.9 %convert_add_fusion.1 = f32[8,80,1024]{2,1,0:T(8,128)S(1)} fusion(bf16[8,80,1024]{2,1,0:T(8,128)(2,1)} %get-tuple-element.11, bf16[8,80,1024]{2,1,0:T(8,128)(2,1)S(1)} %get-tuple-element.10), kind=kLoop, calls=%fused_computation.23 | loop fusion | flops 1966080 | bytes 5242880 | tf_op jit(solution)/shard_map/add | solution.py:241
  148.8 0.0 copy-start.6
  148.8 0.9 fusion.13
  149.8 0.3 collective-permute-start.2
  150.0 0.4 copy-done.6
  150.5 3.1 %fusion.15 = f32[1792,1024]{1,0:T(8,128)S(1)} fusion(bf16[640,1024]{1,0:T(8,128)(2,1)S(1)} %fusion.13, bf16[1,640,1792]{2,1,0:T(8,128)(2,1)S(1)} %copy-done.6), kind=kOutput, calls=%fused_computation.25 | convolution fusion | flops 2348810240 | bytes 10944512 | tf_op jit(solution)/shard_map/dot_general | solution.py:16
  153.6 0.4 convert_reduce_fusion
  154.0 1.2 copy-done.10
  155.2 3.1 %fusion.21 = f32[1024,1792,1]{1,0,2:T(8,128)S(1)} fusion(bf16[8,80,1024]{2,1,0:T(8,128)(2,1)S(1)} %get-tuple-element.14, bf16[8,80,1792]{2,1,0:T(8,128)(2,1)S(1)} %copy-done.10), kind=kOutput, calls=%fused_computation.35 | convolution fusion | flops 2348810240 | bytes 10944512 | tf_op jit(solution)/shard_map/dot_general | solution.py:16
  158.4 7.2 %fusion.9 = bf16[1024,1,1792]{2,0,1:T(8,128)(2,1)} fusion(f32[1024]{0:T(1024)S(1)} %add_multiply_fusion, bf16[8,80,1024]{2,1,0:T(8,128)(2,1)S(1)} %get-tuple-element.16, bf16[8,80,1792]{2,1,0:T(8,128)(2,1)} %get-tuple-element.17, f32[1024,1792,1]{1,0,2:T(8,128)S(1)} %fusion.21, bf16[1024,1,1792]{2,0,1:T(8,128)(2,1)S(1)} %copy-done.4), kind=kOutput, calls=%fused_computation.13 | convolution fusion | flops 2359820288 | bytes 18288640 | tf_op jit(solution)/shard_map/dot_general | solution.py:16
  165.5 4.7 %fusion.8 = bf16[1,1792,1024]{2,1,0:T(8,128)(2,1)} fusion(f32[1792,1024]{1,0:T(8,128)S(1)} %fusion.15, bf16[640,1792]{1,0:T(8,128)(2,1)S(1)} %copy-done.9, bf16[640,1024]{1,0:T(8,128)(2,1)S(1)} %collective-permute-done.2), kind=kOutput, calls=%fused_computation.12 | convolution fusion | flops 2352480256 | bytes 14614528 | tf_op jit(solution)/shard_map/dot_general | solution.py:16
  (20 shorter events, 0.1 us)
Async XLA Ops:
  0.6 10.5 %copy-start = (f32[1,3584]{1,0:T(1,128)S(1)}, f32[1,3584]{1,0:T(1,128)}, u32[]{:S(2)}) copy-start(f32[1,3584]{1,0:T(1,128)} %param.9) | copy-start | bytes 43012
  0.7 7.4 %copy-start.7 = (bf16[1,1792,1024]{2,1,0:T(8,128)(2,1)S(1)}, bf16[1,1792,1024]{2,1,0:T(8,128)(2,1)}, u32[]{:S(2)}) copy-start(bf16[1,1792,1024]{2,1,0:T(8,128)(2,1)} %param.6) | copy-start | bytes 11010052
  3.5 8.4 %copy-start.5 = (bf16[1,640,1792]{2,1,0:T(8,128)(2,1)}, bf16[1,640,1792]{2,1,0:T(8,128)(2,1)S(1)}, u32[]{:S(2)}) copy-start(bf16[1,640,1792]{2,1,0:T(8,128)(2,1)S(1)} %get-tuple-element.19) | copy-start | bytes 6881284
  3.5 7.6 %copy-start.3 = (bf16[1024,1,1792]{2,0,1:T(8,128)(2,1)S(1)}, bf16[1024,1,1792]{2,0,1:T(8,128)(2,1)}, u32[]{:S(2)}) copy-start(bf16[1024,1,1792]{2,0,1:T(8,128)(2,1)} %param.8) | copy-start | bytes 11010052
  3.5 4.6 %collective-permute-start = (bf16[640,1792]{1,0:T(8,128)(2,1)S(1)}, bf16[640,1792]{1,0:T(8,128)(2,1)S(1)}, u32[]{:S(2)}, u32[]{:S(2)}) collective-permute-start(bf16[640,1792]{1,0:T(8,128)(2,1)S(1)} %get-tuple-element.18), channel_id=1, source_target_pairs={{0,1},{1,0},{2,3},{3,2},{4,5},{5,4},{6,7},{7,6},{8,9},{9,8},{10,11... | collective-permute-start | bytes 6881288 | tf_op jit(solution)/shard_map/ppermute | solution.py:20
  8.1 2.6 %copy-start.8 = (bf16[640,1792]{1,0:T(8,128)(2,1)}, bf16[640,1792]{1,0:T(8,128)(2,1)S(1)}, u32[]{:S(2)}) copy-start(bf16[640,1792]{1,0:T(8,128)(2,1)S(1)} %collective-permute-done) | copy-start | bytes 6881284
  10.6 3.8 %collective-permute-start.1 = (bf16[640,1024]{1,0:T(8,128)(2,1)S(1)}, bf16[640,1024]{1,0:T(8,128)(2,1)S(1)}, u32[]{:S(2)}, u32[]{:S(2)}) collective-permute-start(bf16[640,1024]{1,0:T(8,128)(2,1)S(1)} %fusion.18), channel_id=1, source_target_pairs={{0,1},{1,0},{2,3},{3,2},{4,5},{5,4},{6,7},{7,6},{8,9},{9,8},{10,11... | collective-permute-start | bytes 3932168 | tf_op jit(solution)/shard_map/ppermute | solution.py:20
  14.4 1.6 copy-start.1
  146.9 1.9 %copy-start.2 = (bf16[640,1024]{1,0:T(8,128)(2,1)S(1)}, bf16[640,1024]{1,0:T(8,128)(2,1)}, u32[]{:S(2)}) copy-start(bf16[640,1024]{1,0:T(8,128)(2,1)} %add_convert_fusion.1) | copy-start | bytes 3932164
  148.8 1.6 copy-start.6
  149.8 15.8 %collective-permute-start.2 = (bf16[640,1024]{1,0:T(8,128)(2,1)S(1)}, bf16[640,1024]{1,0:T(8,128)(2,1)S(1)}, u32[]{:S(2)}, u32[]{:S(2)}) collective-permute-start(bf16[640,1024]{1,0:T(8,128)(2,1)S(1)} %fusion.13), channel_id=1, source_target_pairs={{0,1},{1,0},{2,3},{3,2},{4,5},{5,4},{6,7},{7,6},{8,9},{9,8},{10,11... | collective-permute-start | bytes 3932168 | tf_op jit(solution)/shard_map/ppermute | solution.py:20
  153.5 1.6 copy-start.10
  155.2 3.2 %copy-start.4 = (bf16[1024,1,1792]{2,0,1:T(8,128)(2,1)S(1)}, bf16[1024,1,1792]{2,0,1:T(8,128)(2,1)}, u32[]{:S(2)}) copy-start(bf16[1024,1,1792]{2,0,1:T(8,128)(2,1)} %param.8) | copy-start | bytes 11010052
  158.4 7.2 %copy-start.9 = (bf16[640,1792]{1,0:T(8,128)(2,1)S(1)}, bf16[640,1792]{1,0:T(8,128)(2,1)}, u32[]{:S(2)}) copy-start(bf16[640,1792]{1,0:T(8,128)(2,1)} %copy-done.8) | copy-start | bytes 6881284
